TPU v7x, 32 devices: a whole 2x2x4 slice. The times are simulated.
32 devices in a mesh: region: 8 (over y, x, core), shard: 4 (over z).
Axes of the slice: x: 2, y: 2, z: 4, core: 2. Of those that a mesh axis runs over, the one named last changes fastest.
Arguments:
- planes: bfloat16 [4, 1024, 512], P(None, ('region', 'shard')), may hold values from -6 to 6
- sed_weights: float32 [6, 4], replicated, may hold values from 0.1 to 2
- psf_taps: float32 [2, 6, 3, 25], replicated, may hold values from 0.004 to 0.08
- resample_rows: bfloat16 [1024, 128, 128], P(('region', 'shard')), may hold values from -0.5 to 0.5
- resample_cols: bfloat16 [1024, 128, 256], P(('region', 'shard')), may hold values from -0.375 to 0.375
- observed: bfloat16 [1024, 128, 128], P(('region', 'shard')), may hold values from -6 to 6
- exposure_meta: int32 [3, 1024], P(None, 'region'), may hold values from 0 to 5, as said below
- slot_counts: int32 [8, 4], P('region'), may hold values from 8 to 32, as said below
Outputs:
- plane_grad: float32 [4, 1024, 512], P(None, ('region', 'shard'))
Inputs may be any that keep to these rules, and one draw needn't show every extreme that they name: `exposure_meta`: row 0 is a row tile of the exposure's region, 0 to 3; row 1 a column tile, 0 to 1; row 2 a band, 0 to 5. `slot_counts`: the live slots of a device are its first ones. In every region one device has all 32 slots live, the others between 8 and 16.
All inputs are finite; a program needn't handle non-finite values.
Results may differ from a plain program's by a relative error of at most 0.003.
Values may be sent and summed in bfloat16 or wider, within the bound.
No kernel may reach another device: no remote copies, remote signals or barrier semaphores. Data moves between devices by JAX's collectives and lax.ppermute only.
A program may use at most 64 MiB of HBM per device.

v0:
```python
import jax
import jax.numpy as jnp
from jax import lax
from jax.sharding import PartitionSpec as P

GROUP = 4


def passed_along(block, axis, distance):
    devices = range(lax.axis_size(axis))
    route = [(i - distance, i) for i in devices if i - distance in devices]
    return lax.ppermute(block, axis, route)


def band_tables(taps, width):
    tap_count = taps.shape[-1]
    offset = (
        jnp.arange(width, dtype=jnp.int32)[:, None]
        - jnp.arange(width, dtype=jnp.int32)[None, :]
        + tap_count // 2
    )
    selector = (offset[None, :, :] == jnp.arange(tap_count, dtype=jnp.int32)[:, None, None]).astype(
        jnp.float32
    )
    return jnp.einsum("btk,kij->btij", taps, selector, precision=lax.Precision.HIGHEST).astype(
        jnp.bfloat16
    )


def local(
    planes,
    sed_weights,
    psf_taps,
    resample_rows,
    resample_cols,
    observed,
    exposure_meta,
    slot_counts,
):
    shard_count = lax.axis_size("shard")
    my_index = lax.axis_index("shard")
    channel_count, tile_rows, col_total = planes.shape
    slot_count, out_rows, win_rows = resample_rows.shape
    win_cols = resample_cols.shape[2]
    region_rows = tile_rows * shard_count
    rim_rows = win_rows - tile_rows
    gathered = lax.all_gather(planes, "shard", axis=1, tiled=True)
    next_part = passed_along(gathered[:, :rim_rows], "region", -1)
    extended = jnp.concatenate([gathered, next_part], axis=1)
    rows_tab = band_tables(psf_taps[0], win_rows)
    cols_tab = band_tables(psf_taps[1], win_cols)
    live_counts = slot_counts[0]
    device_ids = jnp.arange(shard_count, dtype=jnp.int32)
    position = jnp.arange(slot_count, dtype=jnp.int32)
    my_count = jnp.sum(jnp.where(device_ids == my_index, live_counts, 0))
    row_maps, col_maps, pixel_sets = (resample_rows, resample_cols, observed)
    is_live = position < my_count
    region_slot = my_index * slot_count + position
    meta_total = exposure_meta.shape[1]
    matches = (jnp.arange(meta_total, dtype=jnp.int32)[:, None] == region_slot[None, :]).astype(
        jnp.int32
    )
    meta_sel = jnp.dot(exposure_meta, matches)
    live_rank = jnp.cumsum(is_live.astype(jnp.int32)) - 1
    picks = jnp.logical_and(is_live[:, None], live_rank[:, None] == position[None, :])
    live_order = jnp.sum(jnp.where(picks, position[:, None], 0), axis=0)
    live_total = jnp.sum(is_live.astype(jnp.int32))
    turn_total = (live_total + GROUP - 1) // GROUP

    def cut_window(start_row, start_col):
        return lax.dynamic_slice(
            extended, (jnp.int32(0), start_row, start_col), (channel_count, win_rows, win_cols)
        )

    def visit(turn_index, gradient):
        ranks = turn_index * GROUP + jnp.arange(GROUP, dtype=jnp.int32)
        usable = ranks < live_total
        chosen = jnp.take(live_order, jnp.minimum(ranks, slot_count - 1))
        row_start = jnp.take(meta_sel[0], chosen) * tile_rows
        col_start = jnp.take(meta_sel[1], chosen) * win_cols
        band_of = jnp.take(meta_sel[2], chosen)
        windows = jax.vmap(cut_window)(row_start, col_start)
        sed_sel = jnp.take(sed_weights, band_of, axis=0)
        py_mat = jnp.take(rows_tab, band_of, axis=0)
        px_mat = jnp.take(cols_tab, band_of, axis=0)
        ry_mat = jnp.take(row_maps, chosen, axis=0)
        rx_mat = jnp.take(col_maps, chosen, axis=0)
        pixels = jnp.take(pixel_sets, chosen, axis=0)
        mixed = jnp.sum(sed_sel[:, :, None, None] * windows.astype(jnp.float32), axis=1).astype(
            jnp.bfloat16
        )
        smeared = jnp.einsum(
            "gtiy,gyx->gtix", py_mat, mixed, preferred_element_type=jnp.float32
        ).astype(jnp.bfloat16)
        blurred = jnp.einsum(
            "gtix,gtjx->gij", smeared, px_mat, preferred_element_type=jnp.float32
        ).astype(jnp.bfloat16)
        sampled = jnp.einsum(
            "goy,gyx->gox", ry_mat, blurred, preferred_element_type=jnp.float32
        ).astype(jnp.bfloat16)
        model = jnp.einsum("gox,gpx->gop", sampled, rx_mat, preferred_element_type=jnp.float32)
        misfit = (model - pixels.astype(jnp.float32)).astype(jnp.bfloat16)
        back_rows = jnp.einsum(
            "goy,gop->gyp", ry_mat, misfit, preferred_element_type=jnp.float32
        ).astype(jnp.bfloat16)
        back = jnp.einsum(
            "gyp,gpx->gyx", back_rows, rx_mat, preferred_element_type=jnp.float32
        ).astype(jnp.bfloat16)
        unsmeared = jnp.einsum(
            "gtiy,gix->gtyx", py_mat, back, preferred_element_type=jnp.float32
        ).astype(jnp.bfloat16)
        window_grad = jnp.einsum(
            "gtyj,gtjx->gyx", unsmeared, px_mat, preferred_element_type=jnp.float32
        )
        contrib = sed_sel[:, :, None, None] * window_grad[:, None]
        for member in range(GROUP):
            corner = (jnp.int32(0), row_start[member], col_start[member])
            current = lax.dynamic_slice(gradient, corner, (channel_count, win_rows, win_cols))
            added = jnp.where(usable[member], contrib[member], 0.0)
            gradient = lax.dynamic_update_slice(gradient, current + added, corner)
        return gradient

    start = jnp.zeros((channel_count, region_rows + rim_rows, col_total), jnp.float32)
    gradient = lax.fori_loop(0, turn_total, visit, start)
    incoming = passed_along(gradient[:, region_rows:], "region", 1)
    own_rows = gradient[:, :region_rows].at[:, :rim_rows].add(incoming)
    return lax.psum_scatter(own_rows, "shard", scatter_dimension=1, tiled=True)


def solution(mesh):
    placed = (
        P(None, ("region", "shard"), None),
        P(),
        P(),
        P(("region", "shard"), None, None),
        P(("region", "shard"), None, None),
        P(("region", "shard"), None, None),
        P(None, "region"),
        P("region", None),
    )
    return jax.shard_map(
        local,
        mesh=mesh,
        in_specs=placed,
        out_specs=P(None, ("region", "shard"), None),
        check_vma=False,
    )
```

profile of v0, /device:TPU:10, one launch (start us, length us, event | category | flops | bytes accessed | tf_op | source)
XLA Modules:
  0.0 723.3 jit_solution(6760753931080793872)
XLA Ops:
  6.5 16.8 %all_gather.3 = bf16[4,128,512]{2,1,0:T(8,128)(2,1)S(1)} all-gather(bf16[4,32,512]{2,1,0:T(8,128)(2,1)} %param.16), channel_id=1, replica_groups=mesh['region'=8,'shard'=4] {'shard'}, dimensions={1}, use_global_device_ids=true | all-gather | bytes 655360 | tf_op jit(solution)/shard_map/all_gather | solution.py:47
  24.9 1.9 collective-permute-start
  31.5 3.9 convert_bitcast_fusion
  37.6 2.1 copy.27
  39.7 1.9 copy.28
  45.2 236.9 %while.14 = (s32[]{:T(128)}, f32[4,224,512]{2,1,0:T(8,128)}, s32[]{:T(128)}, s32[3,32]{1,0:T(4,128)}, s32[32]{0:T(128)S(1)}, /*index=5*/s32[]{:T(128)}, f32[6,4]...) while((s32[]{:T(128)}, f32[4,224,512]{2,1,0:T(8,128)}, ...), condition=%wide.region_6.9_spmd, body=%wide.region_4.8_spmd.sunk | while | flops 728304896 | bytes 28474076 | solution.py:124
  69.8 2.4 gather_fusion.7
  72.3 2.2 gather_fusion.8
  76.2 8.8 %while.15 = (s32[]{:T(128)}, bf16[4,224,512]{2,1,0:T(8,128)(2,1)S(1)}, s32[4,3]{1,0:T(4,128)S(1)}, bf16[4,4,128,256]{3,2,1,0:T(8,128)(2,1)S(1)}, s32[]{:T(128)}) while((s32[]{:T(128)}, bf16[4,224,512]{2,1,0:T(8,128)(2,1)S(1)}, s32[4,3]{1,0:T(4,128)S(1)}, bf16[4,4,128,256]{3,2,1,0:T(8,128)(2,1)S(1)}, s32[]{:T(128)}) %tuple.81), condition=%wide.while_cond.1, body=%wide.while_body.1.sunk | while | flops 2 | bytes 524413 | solution.py:71
  85.2 2.4 gather_fusion.2
  87.7 2.2 fusion.83
  95.3 2.0 fusion.90
  97.3 5.5 dynamic_update_slice.16
  102.8 1.9 fusion.91
  104.7 5.0 dynamic_update_slice.17
  109.8 1.9 fusion.92
  111.7 5.1 dynamic_update_slice.18
  116.8 2.0 fusion.93
  118.8 4.9 dynamic_update_slice.19
  148.3 2.4 gather_fusion.7
  150.8 2.2 gather_fusion.8
  154.6 8.8 %while.15 = (s32[]{:T(128)}, bf16[4,224,512]{2,1,0:T(8,128)(2,1)S(1)}, s32[4,3]{1,0:T(4,128)S(1)}, bf16[4,4,128,256]{3,2,1,0:T(8,128)(2,1)S(1)}, s32[]{:T(128)}) while((s32[]{:T(128)}, bf16[4,224,512]{2,1,0:T(8,128)(2,1)S(1)}, s32[4,3]{1,0:T(4,128)S(1)}, bf16[4,4,128,256]{3,2,1,0:T(8,128)(2,1)S(1)}, s32[]{:T(128)}) %tuple.81), condition=%wide.while_cond.1, body=%wide.while_body.1.sunk | while | flops 2 | bytes 524413 | solution.py:71
  163.7 2.4 gather_fusion.2
  166.2 2.2 fusion.83
  173.8 2.0 fusion.90
  175.8 4.3 dynamic_update_slice.16
  180.2 1.9 fusion.91
  182.1 4.9 dynamic_update_slice.17
  186.9 1.9 fusion.92
  188.9 5.1 dynamic_update_slice.18
  194.0 2.1 fusion.93
  196.1 5.8 dynamic_update_slice.19
  226.5 2.4 gather_fusion.7
  229.0 2.2 gather_fusion.8
  232.9 8.8 %while.15 = (s32[]{:T(128)}, bf16[4,224,512]{2,1,0:T(8,128)(2,1)S(1)}, s32[4,3]{1,0:T(4,128)S(1)}, bf16[4,4,128,256]{3,2,1,0:T(8,128)(2,1)S(1)}, s32[]{:T(128)}) while((s32[]{:T(128)}, bf16[4,224,512]{2,1,0:T(8,128)(2,1)S(1)}, s32[4,3]{1,0:T(4,128)S(1)}, bf16[4,4,128,256]{3,2,1,0:T(8,128)(2,1)S(1)}, s32[]{:T(128)}) %tuple.81), condition=%wide.while_cond.1, body=%wide.while_body.1.sunk | while | flops 2 | bytes 524413 | solution.py:71
  241.9 2.4 gather_fusion.2
  244.4 2.2 fusion.83
  252.0 2.0 fusion.90
  254.0 5.5 dynamic_update_slice.16
  259.5 2.0 fusion.91
  261.5 5.5 dynamic_update_slice.17
  267.0 2.0 fusion.92
  269.0 5.5 dynamic_update_slice.18
  274.5 2.1 fusion.93
  276.6 5.5 dynamic_update_slice.19
  283.2 1.9 collective-permute-start.1
  286.5 90.4 %collective-permute-done.1 = f32[4,96,512]{2,1,0:T(8,128)S(1)} collective-permute-done((f32[4,96,512]{2,1,0:T(8,128)S(1)}, f32[4,96,512]{2,1,0:T(8,128)S(1)}, u32[]{:S(2)}, u32[]{:S(2)}) %collective-permute-start.1) | collective-permute-done | bytes 786464 | tf_op jit(solution)/shard_map/ppermute | solution.py:12
  379.2 337.2 %reduce-scatter.2.cloned.1.call-done = f32[4,32,512]{2,1,0:T(8,128)} async-done(((f32[4,128,512]{2,1,0:T(8,128)}), f32[4,32,512]{2,1,0:T(8,128)}) %reduce-scatter.2.cloned.1.call-update) | async-done | bytes 262160 | tf_op jit(solution)/shard_map/reduce_scatter | solution.py:127
  (171 shorter events, 91.6 us)
Async XLA Ops:
  6.5 35.2 %copy-start = (s32[3,128]{1,0:T(4,128)S(1)}, s32[3,128]{1,0:T(4,128)}, u32[]{:S(2)}) copy-start(s32[3,128]{1,0:T(4,128)} %param.22) | copy-start | bytes 4612
  6.5 23.1 %copy-start.6 = (f32[2,6,3,25]{3,0,2,1:T(2,128)S(1)}, f32[2,6,3,25]{3,0,2,1:T(2,128)}, u32[]{:S(2)}) copy-start(f32[2,6,3,25]{3,0,2,1:T(2,128)} %param.18) | copy-start | bytes 10804
  6.5 709.9 %reduce-scatter.2.cloned.1.call-start = ((), (), s32[]{:S(2)}) async-start(), calls=%async_computation.1 | async-start | bytes 1310720 | tf_op jit(solution)/shard_map/reduce_scatter | solution.py:127
  23.3 0.8 copy-start.3
  24.9 17.6 %collective-permute-start = (bf16[4,96,512]{2,1,0:T(8,128)(2,1)}, bf16[4,96,512]{2,1,0:T(8,128)(2,1)}, u32[]{:S(2)}, u32[]{:S(2)}) collective-permute-start(bf16[4,96,512]{2,1,0:T(8,128)(2,1)} %slice.142), channel_id=1, source_target_pairs={{4,0},{8,4},{12,8},{16,12},{20,16},{24,20},{28,24},{5,1},{9,5},{13... | collective-permute-start | bytes 1179656 | tf_op jit(solution)/shard_map/ppermute | solution.py:12
  31.5 6.0 copy-start.7
  50.5 25.7 %copy-start.5 = (pred[4]{0:T(512)(128)(4,1)}, pred[4]{0:T(512)(128)(4,1)S(1)}, u32[]{:S(2)}) copy-start(pred[4]{0:T(512)(128)(4,1)S(1)} %get-tuple-element.350) | copy-start | bytes 16 | tf_op jit(solution)/shard_map/while
  67.4 8.8 %copy-start.4 = (s32[1024]{0:T(1024)}, s32[1024]{0:T(1024)S(1)}, u32[]{:S(2)}) copy-start(s32[1024]{0:T(1024)S(1)} %pad_clamp_fusion.8) | copy-start | bytes 12292 | tf_op jit(solution)/shard_map/while
  76.1 11.5 %copy-start.1 = (bf16[4,3,128,128]{3,2,1,0:T(8,128)(2,1)}, bf16[4,3,128,128]{3,2,1,0:T(8,128)(2,1)S(1)}, u32[]{:S(2)}) copy-start(bf16[4,3,128,128]{3,2,1,0:T(8,128)(2,1)S(1)} %gather_fusion.6) | copy-start | bytes 1179652 | tf_op jit(solution)/shard_map/while
  128.9 25.7 %copy-start.5 = (pred[4]{0:T(512)(128)(4,1)}, pred[4]{0:T(512)(128)(4,1)S(1)}, u32[]{:S(2)}) copy-start(pred[4]{0:T(512)(128)(4,1)S(1)} %get-tuple-element.350) | copy-start | bytes 16 | tf_op jit(solution)/shard_map/while
  145.9 8.8 %copy-start.4 = (s32[1024]{0:T(1024)}, s32[1024]{0:T(1024)S(1)}, u32[]{:S(2)}) copy-start(s32[1024]{0:T(1024)S(1)} %pad_clamp_fusion.8) | copy-start | bytes 12292 | tf_op jit(solution)/shard_map/while
  154.6 11.5 %copy-start.1 = (bf16[4,3,128,128]{3,2,1,0:T(8,128)(2,1)}, bf16[4,3,128,128]{3,2,1,0:T(8,128)(2,1)S(1)}, u32[]{:S(2)}) copy-start(bf16[4,3,128,128]{3,2,1,0:T(8,128)(2,1)S(1)} %gather_fusion.6) | copy-start | bytes 1179652 | tf_op jit(solution)/shard_map/while
  207.1 25.7 %copy-start.5 = (pred[4]{0:T(512)(128)(4,1)}, pred[4]{0:T(512)(128)(4,1)S(1)}, u32[]{:S(2)}) copy-start(pred[4]{0:T(512)(128)(4,1)S(1)} %get-tuple-element.350) | copy-start | bytes 16 | tf_op jit(solution)/shard_map/while
  224.1 8.8 %copy-start.4 = (s32[1024]{0:T(1024)}, s32[1024]{0:T(1024)S(1)}, u32[]{:S(2)}) copy-start(s32[1024]{0:T(1024)S(1)} %pad_clamp_fusion.8) | copy-start | bytes 12292 | tf_op jit(solution)/shard_map/while
  232.8 11.5 %copy-start.1 = (bf16[4,3,128,128]{3,2,1,0:T(8,128)(2,1)}, bf16[4,3,128,128]{3,2,1,0:T(8,128)(2,1)S(1)}, u32[]{:S(2)}) copy-start(bf16[4,3,128,128]{3,2,1,0:T(8,128)(2,1)S(1)} %gather_fusion.6) | copy-start | bytes 1179652 | tf_op jit(solution)/shard_map/while
  283.2 93.6 %collective-permute-start.1 = (f32[4,96,512]{2,1,0:T(8,128)S(1)}, f32[4,96,512]{2,1,0:T(8,128)S(1)}, u32[]{:S(2)}, u32[]{:S(2)}) collective-permute-start(f32[4,96,512]{2,1,0:T(8,128)S(1)} %slice.102), channel_id=1, source_target_pairs={{0,4},{4,8},{8,12},{12,16},{16,20},{20,24},{24,28},{1,5},{5,9},{9,... | collective-permute-start | bytes 2359304 | tf_op jit(solution)/shard_map/ppermute | solution.py:12
  378.2 1.0 copy-start.2
Sparse Core Ops, SparseCore 0:
  379.3 337.0 reduce-scatter.1
where the time goes:
time: 737 us; the launch traced here: 723 us
  waiting for transfers between devices  428 us (58%)
  local copies, waits for them, and re-layouts  149 us (20%)
  loops' own time  47 us (6%)
  other arithmetic  36.5 us (5%)
  matrix products  28.5 us (4%)
  blocking collectives  16.8 us (2%)
  between operations  14.2 us (2%)
    reduce_scatter x1, waiting for transfers between devices, local(): return lax.psum_scatter(own_rows, 'shard', scatter_dimension=1, tiled=True)  337 us
    ppermute x2, waiting for transfers between devices, passed_along(): return lax.ppermute(block, axis, route)  90.4 us
    dynamic_update_slice x12, local copies, waits for them, and re-layouts, visit(): gradient = lax.dynamic_update_slice(gradient, current + added, corner)  62.6 us
    another operation x1, loops' own time, local(): gradient = lax.fori_loop(0, turn_total, visit, start)  46.7 us
    gather x36, local copies, waits for them, and re-layouts  26 us
    add x12, other arithmetic, visit(): gradient = lax.dynamic_update_slice(gradient, current + added, corner)  23.8 us
    all_gather x1, blocking collectives, local(): gathered = lax.all_gather(planes, 'shard', axis=1, tiled=True)  16.8 us
  transfers between devices with their start and end apart: 3, of which 2 were waited for; matrix products, arithmetic and copies ran while one was open for 2% of the time, Pallas kernels for 0%

commit v1 on v0

v1 whole, which is shorter than its diff:
```python
import functools

import jax
import jax.numpy as jnp
from jax import lax
from jax.experimental import pallas as pl
from jax.experimental.pallas import tpu as pltpu
from jax.sharding import PartitionSpec as P

GROUP = 4


def shifted(block, axis, distance):
    size = lax.axis_size(axis)
    return lax.ppermute(block, axis, [(i, (i + distance) % size) for i in range(size)])


def passed_along(block, axis, distance):
    devices = range(lax.axis_size(axis))
    route = [(i - distance, i) for i in devices if i - distance in devices]
    return lax.ppermute(block, axis, route)


def band_tables(taps, width):
    tap_count = taps.shape[-1]
    offset = (
        jnp.arange(width, dtype=jnp.int32)[:, None]
        - jnp.arange(width, dtype=jnp.int32)[None, :]
        + tap_count // 2
    )
    selector = (offset[None, :, :] == jnp.arange(tap_count, dtype=jnp.int32)[:, None, None]).astype(
        jnp.float32
    )
    table = jnp.einsum("btk,kij->btij", taps, selector, precision=lax.Precision.HIGHEST)
    bands, terms = taps.shape[:2]
    return table.astype(jnp.bfloat16).reshape(bands, terms * width, width)


def dot(a, b, contract):
    return lax.dot_general(a, b, ((contract[:1], contract[1:]), ((), ())), preferred_element_type=jnp.float32)


def exposures_kernel(
    terms,
    tile_rows,
    count_ref,
    row_tile_ref,
    col_tile_ref,
    band_ref,
    sed_ref,
    ext_ref,
    py_ref,
    py_t_ref,
    px_ref,
    px_t_ref,
    ry_hbm,
    rx_hbm,
    obs_hbm,
    grad_ref,
    ry_ref,
    rx_ref,
    obs_ref,
    sems,
):
    channels, ext_rows, cols = ext_ref.shape
    slots, out_rows, win_rows = ry_hbm.shape
    win_cols = rx_hbm.shape[2]
    count = count_ref[0]
    turns = (count + GROUP - 1) // GROUP

    def copies(slot):
        return [
            pltpu.make_async_copy(hbm.at[slot], vmem.at[slot], sems.at[i, slot])
            for i, (hbm, vmem) in enumerate(((ry_hbm, ry_ref), (rx_hbm, rx_ref), (obs_hbm, obs_ref)))
        ]

    def fetch(slot, carry):
        for copy in copies(slot):
            copy.start()
        return carry

    lax.fori_loop(0, turns * GROUP, fetch, 0)
    grad_ref[...] = jnp.zeros_like(grad_ref)

    def visit(turn, carry):
        slot_of = [turn * GROUP + m for m in range(GROUP)]
        band = [band_ref[s] for s in slot_of]
        row = [pl.multiple_of(row_tile_ref[s] * tile_rows, tile_rows) for s in slot_of]
        col = [pl.multiple_of(col_tile_ref[s] * win_cols, win_cols) for s in slot_of]
        live = [(s < count).astype(jnp.float32) for s in slot_of]
        weight = [[sed_ref[b, k] for k in range(channels)] for b in band]
        for s in slot_of:
            for copy in copies(s):
                copy.wait()
        mixed = []
        for m in range(GROUP):
            total = None
            for k in range(channels):
                window = ext_ref[k, pl.ds(row[m], win_rows), pl.ds(col[m], win_cols)]
                term = weight[m][k] * window.astype(jnp.float32)
                total = term if total is None else total + term
            mixed.append(total.astype(jnp.bfloat16))
        smeared = [dot(py_ref[band[m]], mixed[m], (1, 0)).astype(jnp.bfloat16) for m in range(GROUP)]
        blurred = []
        for m in range(GROUP):
            wide = jnp.concatenate([smeared[m][t * win_rows : (t + 1) * win_rows] for t in range(terms)], axis=1)
            blurred.append(dot(wide, px_t_ref[band[m]], (1, 0)).astype(jnp.bfloat16))
        sampled = [dot(ry_ref[slot_of[m]], blurred[m], (1, 0)).astype(jnp.bfloat16) for m in range(GROUP)]
        model = [dot(sampled[m], rx_ref[slot_of[m]], (1, 1)) for m in range(GROUP)]
        misfit = [
            (model[m] - obs_ref[slot_of[m]].astype(jnp.float32)).astype(jnp.bfloat16) for m in range(GROUP)
        ]
        back_rows = [dot(ry_ref[slot_of[m]], misfit[m], (0, 0)).astype(jnp.bfloat16) for m in range(GROUP)]
        back = [dot(back_rows[m], rx_ref[slot_of[m]], (1, 0)).astype(jnp.bfloat16) for m in range(GROUP)]
        unsmeared = [dot(py_t_ref[band[m]], back[m], (1, 0)).astype(jnp.bfloat16) for m in range(GROUP)]
        for m in range(GROUP):
            wide = jnp.concatenate([unsmeared[m][t * win_rows : (t + 1) * win_rows] for t in range(terms)], axis=1)
            window_grad = dot(wide, px_ref[band[m]], (1, 0))
            for k in range(channels):
                place = (k, pl.ds(row[m], win_rows), pl.ds(col[m], win_cols))
                grad_ref[place] = grad_ref[place] + (weight[m][k] * live[m]) * window_grad
        return carry

    lax.fori_loop(0, turns, visit, 0)


def local(
    planes,
    sed_weights,
    psf_taps,
    resample_rows,
    resample_cols,
    observed,
    exposure_meta,
    slot_counts,
):
    shard_count = lax.axis_size("shard")
    my_index = lax.axis_index("shard")
    channel_count, tile_rows, col_total = planes.shape
    slot_count, out_rows, win_rows = resample_rows.shape
    win_cols = resample_cols.shape[2]
    region_rows = tile_rows * shard_count
    rim_rows = win_rows - tile_rows
    terms = psf_taps.shape[2]
    gathered = lax.all_gather(planes, "shard", axis=1, tiled=True)
    next_part = passed_along(gathered[:, :rim_rows], "region", -1)
    extended = jnp.concatenate([gathered, next_part], axis=1)
    py = band_tables(psf_taps[0], win_rows)
    py_t = band_tables(psf_taps[0, :, :, ::-1], win_rows)
    px = band_tables(psf_taps[1], win_cols)
    px_t = band_tables(psf_taps[1, :, :, ::-1], win_cols)
    count = lax.dynamic_slice(slot_counts[0], (my_index,), (1,))
    meta = lax.dynamic_slice(exposure_meta, (jnp.int32(0), my_index * slot_count), (3, slot_count))

    smem = pl.BlockSpec(memory_space=pltpu.SMEM)
    vmem = pl.BlockSpec(memory_space=pltpu.VMEM)
    anywhere = pl.BlockSpec(memory_space=pl.ANY)
    gradient = pl.pallas_call(
        functools.partial(exposures_kernel, terms, tile_rows),
        out_shape=jax.ShapeDtypeStruct((channel_count, region_rows + rim_rows, col_total), jnp.float32),
        in_specs=[smem] * 5 + [vmem] * 5 + [anywhere] * 3,
        out_specs=vmem,
        scratch_shapes=[
            pltpu.VMEM((slot_count, out_rows, win_rows), jnp.bfloat16),
            pltpu.VMEM((slot_count, out_rows, win_cols), jnp.bfloat16),
            pltpu.VMEM((slot_count, out_rows, out_rows), jnp.bfloat16),
            pltpu.SemaphoreType.DMA((3, slot_count)),
        ],
        compiler_params=pltpu.CompilerParams(vmem_limit_bytes=48 * 1024 * 1024),
        cost_estimate=pl.CostEstimate(flops=6 * 10**9, bytes_accessed=6 * 10**6, transcendentals=0),
    )(
        count,
        meta[0],
        meta[1],
        meta[2],
        sed_weights,
        extended,
        py,
        py_t,
        px,
        px_t,
        resample_rows,
        resample_cols,
        observed,
    )

    spill = passed_along(gradient[:, region_rows:].astype(jnp.bfloat16), "region", 1)
    own_rows = gradient[:, :region_rows].at[:, :rim_rows].add(spill.astype(jnp.float32))
    result = lax.dynamic_slice(own_rows, (jnp.int32(0), my_index * tile_rows, jnp.int32(0)), planes.shape)
    for step in range(1, shard_count):
        there = lax.rem(my_index + step, shard_count) * tile_rows
        part = lax.dynamic_slice(own_rows, (jnp.int32(0), there, jnp.int32(0)), planes.shape)
        result = result + shifted(part.astype(jnp.bfloat16), "shard", step).astype(jnp.float32)
    return result


def solution(mesh):
    placed = (
        P(None, ("region", "shard"), None),
        P(),
        P(),
        P(("region", "shard"), None, None),
        P(("region", "shard"), None, None),
        P(("region", "shard"), None, None),
        P(None, "region"),
        P("region", None),
    )
    return jax.shard_map(
        local,
        mesh=mesh,
        in_specs=placed,
        out_specs=P(None, ("region", "shard"), None),
        check_vma=False,
    )
```

time: 737 us -> 90.5 us (0.12); the launches traced: 723 us -> 90.6 us
  waiting for transfers between devices: 428 us -> 17.3 us
  local copies, waits for them, and re-layouts: 149 us -> 12.5 us
  loops' own time: 47 us -> 0 us
  other arithmetic: 36.5 us -> 1.97 us
  Pallas kernels: 0 us -> 21.8 us
  matrix products: 28.5 us -> 12.6 us
  between operations: 14.2 us -> 0.18 us
    reduce_scatter x1 -> x0, waiting for transfers between devices: 337 us -> none  [local(): return lax.psum_scatter(own_rows, 'shard', scatter_dimension=1, tiled=True)]
    ppermute x2, waiting for transfers between devices: 90.4 us -> 7.05 us  [passed_along(): return lax.ppermute(block, axis, route)]
    gather x66 -> x0, local copies, waits for them, and re-layouts: 66.8 us -> none
    dynamic_update_slice x12 -> x0, local copies, waits for them, and re-layouts: 62.6 us -> none  [visit(): gradient = lax.dynamic_update_slice(gradient, current + added, corner)]
    another operation x4 -> x0, loops' own time: 47 us -> none  [the longest x1 46.7 us: local(): gradient = lax.fori_loop(0, turn_total, visit, start)]
    add x13 -> x1, other arithmetic: 23.8 us -> 0.77 us  [local(): result + shifted(part.astype(jnp.bfloat16), 'shard', step).astype(jnp.flo...]
    dot_general x13 -> x0, matrix products: 22.8 us -> none  [the longest x3 6.74 us: visit(): jnp.einsum('gtix,gtjx->gij', smeared, px_mat, preferred_element_type=jnp....]
    pallas_call x0 -> x1, Pallas kernels: none -> 21.8 us  [local(): pl.pallas_call(functools.partial(exposures_kernel, terms, tile_rows), out...]
  transfers between devices with their start and end apart: 3 -> 5, of which waited for: 2 -> 4; matrix products, arithmetic and copies ran while one was open for 2% -> 23% of each run, Pallas kernels for 0% -> 0%
where the time goes in v1:
time: 90.5 us; the launch traced here: 90.6 us
  Pallas kernels  21.8 us (24%)
  waiting for transfers between devices  17.3 us (19%)
  blocking collectives  16.8 us (19%)
  matrix products  12.6 us (14%)
  local copies, waits for them, and re-layouts  12.5 us (14%)
  starting transfers between devices  7.34 us (8%)
  other arithmetic  1.97 us (2%)
    pallas_call x1, Pallas kernels, local(): pl.pallas_call(functools.partial(exposures_kernel, terms, tile_rows), out...  21.8 us
    all_gather x1, blocking collectives, local(): gathered = lax.all_gather(planes, 'shard', axis=1, tiled=True)  16.8 us
    dot_general x4, matrix products, band_tables(): jnp.einsum('btk,kij->btij', taps, selector, precision=lax.Precision.HIGHEST)  12.6 us
    ppermute x3, waiting for transfers between devices, shifted(): lax.ppermute(block, axis, [(i, (i + distance) % size) for i in range(size)])  10.3 us
    ppermute x2, waiting for transfers between devices, passed_along(): return lax.ppermute(block, axis, route)  7.05 us
    convert_element_type x4, local copies, waits for them, and re-layouts, band_tables(): return table.astype(jnp.bfloat16).reshape(bands, terms * width, width)  6.06 us
    ppermute x2, starting transfers between devices, passed_along(): return lax.ppermute(block, axis, route)  3.83 us
    unnamed x21, local copies, waits for them, and re-layouts  3.77 us
  transfers between devices with their start and end apart: 5, of which 4 were waited for; matrix products, arithmetic and copies ran while one was open for 23% of the time, Pallas kernels for 0%

profile of v1, /device:TPU:10, one launch (start us, length us, event | category | flops | bytes accessed | tf_op | source)
XLA Modules:
  0.0 90.6 jit_solution(9003960007465991859)
XLA Ops:
  0.0 0.0 copy-start
  0.0 16.8 %all_gather.3 = bf16[4,128,512]{2,1,0:T(8,128)(2,1)S(1)} all-gather(bf16[4,32,512]{2,1,0:T(8,128)(2,1)} %param.10), channel_id=1, replica_groups=mesh['region'=8,'shard'=4] {'shard'}, dimensions={1}, use_global_device_ids=true | all-gather | bytes 655360 | tf_op jit(solution)/shard_map/all_gather | solution.py:145
  16.8 0.0 copy-start.3
  16.8 0.8 copy-done.3
  17.6 0.8 slice.61
  18.4 1.9 %collective-permute-start = (bf16[4,96,512]{2,1,0:T(8,128)(2,1)}, bf16[4,96,512]{2,1,0:T(8,128)(2,1)}, u32[]{:S(2)}, u32[]{:S(2)}) collective-permute-start(bf16[4,96,512]{2,1,0:T(8,128)(2,1)} %slice.61), channel_id=1, source_target_pairs={{4,0},{8,4},{12,8},{16,12},{20,16},{24,20},{28,24},{5,1},{9,5},{13... | collective-permute-start | bytes 1179656 | tf_op jit(solution)/shard_map/ppermute | solution.py:21
  20.4 0.8 fusion.37
  21.2 0.1 rev.7
  21.3 3.9 %convert_bitcast_fusion.1 = bf16[6,3,256,256]{3,0,1,2:T(8,128)(2,1)S(1)} fusion(s32[256,256]{1,0:T(8,128)S(1)} %subtract_add_fusion, f32[1,6,3,25]{3,0,2,1:T(1,128)S(1)} %get-tuple-element.20), kind=kOutput, calls=%fused_computation.7 | convolution fusion | flops 356712448 | bytes 2623240 | tf_op jit(solution)/shard_map/btk,kij->btij/dot_general | solution.py:34
  25.2 5.1 %convert_bitcast_fusion = bf16[6,3,256,256]{3,0,1,2:T(8,128)(2,1)} fusion(s32[256,256]{1,0:T(8,128)S(1)} %subtract_add_fusion, f32[1,6,3,25]{3,1,2,0:T(8,128)S(1)} %rev.7), kind=kOutput, calls=%fused_computation.6 | convolution fusion | flops 356712448 | bytes 2623240 | tf_op jit(solution)/shard_map/btk,kij->btij/dot_general | solution.py:34
  30.3 0.1 rev.6
  30.4 1.8 %fusion.25 = bf16[6,3,128,128]{3,0,1,2:T(8,128)(2,1)} fusion(s32[128,128]{1,0:T(8,128)S(1)} %subtract_add_fusion.1, f32[1,6,3,25]{3,0,2,1:T(1,128)S(1)} %get-tuple-element.21), kind=kOutput, calls=%fused_computation.15 | convolution fusion | flops 89178112 | bytes 657160 | tf_op jit(solution)/shard_map/btk,kij->btij/dot_general | solution.py:34
  32.2 1.8 %fusion.22 = bf16[6,3,128,128]{3,0,1,2:T(8,128)(2,1)} fusion(s32[128,128]{1,0:T(8,128)S(1)} %subtract_add_fusion.1, f32[1,6,3,25]{3,1,2,0:T(8,128)S(1)} %rev.6), kind=kOutput, calls=%fused_computation.14 | convolution fusion | flops 89178112 | bytes 657160 | tf_op jit(solution)/shard_map/btk,kij->btij/dot_general | solution.py:34
  34.0 3.9 %copy.14 = bf16[6,3,256,256]{3,2,1,0:T(8,128)(2,1)} copy(bf16[6,3,256,256]{3,0,1,2:T(8,128)(2,1)} %convert_bitcast_fusion) | data formatting | bytes 4718592 | tf_op jit(solution)/shard_map/convert_element_type | solution.py:36
  37.9 0.0 copy-start.6
  37.9 0.0 copy-start.5
  37.9 2.0 %copy.13 = bf16[6,3,256,256]{3,2,1,0:T(8,128)(2,1)} copy(bf16[6,3,256,256]{3,0,1,2:T(8,128)(2,1)S(1)} %convert_bitcast_fusion.1) | data formatting | bytes 4718592 | tf_op jit(solution)/shard_map/convert_element_type | solution.py:36
  39.9 0.0 copy-done.6
  39.9 0.0 copy-start.7
  39.9 0.1 copy.11
  40.0 0.0 copy-done.5
  40.0 0.1 copy.10
  40.1 0.4 copy-done.7
  40.6 0.1 copy.15.sed_ref
  40.7 0.0 copy-done.8
  40.7 0.6 constant_dynamic-slice_fusion.1
  41.3 0.0 copy-done
  41.3 0.1 constant_dynamic-slice_fusion
  41.3 0.0 collective-permute-done
  41.3 0.0 copy-done.4
  41.3 1.1 %pad_maximum_fusion.ext_ref = bf16[4,224,512]{2,1,0:T(8,128)(2,1)S(1)} fusion(bf16[4,96,512]{2,1,0:T(8,128)(2,1)} %collective-permute-done, bf16[4,128,512]{2,1,0:T(8,128)(2,1)S(1)} %copy-done.4), kind=kLoop, calls=%fused_computation.18 | loop fusion | flops 1835008 | bytes 1835008 | tf_op jit(solution)/shard_map/concatenate | solution.py:147
  42.4 0.0 copy-start.1
  42.4 1.2 %copy-done.1 = bf16[32,128,128]{2,1,0:T(8,128)(2,1)S(1)} copy-done((bf16[32,128,128]{2,1,0:T(8,128)(2,1)S(1)}, bf16[32,128,128]{2,1,0:T(8,128)(2,1)}, u32[]{:S(2)}) %copy-start.1) | copy-done | bytes 1048600
  43.6 1.2 %copy-done.2 = bf16[32,128,128]{2,1,0:T(8,128)(2,1)S(1)} copy-done((bf16[32,128,128]{2,1,0:T(8,128)(2,1)S(1)}, bf16[32,128,128]{2,1,0:T(8,128)(2,1)}, u32[]{:S(2)}) %copy-start.2) | copy-done | bytes 1048600
  44.9 21.8 %shard_map.82 = f32[4,224,512]{2,1,0:T(8,128)S(1)} custom-call(s32[1]{0:T(128)} %bitcast.count_ref, s32[32]{0:T(128)S(1)} %get-tuple-element.24.row_tile_ref, s32[32]{0:T(128)S(1)} %get-tuple-element.23.col_tile_ref, s32[32]{0:T(128)S(1)} %get-tuple-element.22.band_ref, f32[6,4]{1,0:T(8,128)S(1)} %copy.15.sed_ref, ...), custom_call_target="tpu_custom_call" | custom-call | flops 6000000000 | bytes 6000000 | tf_op jit(solution)/shard_map/pallas_call | solution.py:158
  66.7 0.1 slice.72
  66.7 1.9 %collective-permute-start.1 = (bf16[4,96,512]{2,1,0:T(8,128)(2,1)S(1)}, bf16[4,96,512]{2,1,0:T(8,128)(2,1)S(1)}, u32[]{:S(2)}, u32[]{:S(2)}) collective-permute-start(bf16[4,96,512]{2,1,0:T(8,128)(2,1)S(1)} %slice.72), channel_id=1, source_target_pairs={{0,4},{4,8},{8,12},{12,16},{16,20},{20,24},{24,28},{1,5},{5,9},{9,... | collective-permute-start | bytes 1179656 | tf_op jit(solution)/shard_map/ppermute | solution.py:21
  68.7 0.1 slice.62
  68.8 7.0 %collective-permute-done.1 = bf16[4,96,512]{2,1,0:T(8,128)(2,1)S(1)} collective-permute-done((bf16[4,96,512]{2,1,0:T(8,128)(2,1)S(1)}, bf16[4,96,512]{2,1,0:T(8,128)(2,1)S(1)}, u32[]{:S(2)}, u32[]{:S(2)}) %collective-permute-start.1) | collective-permute-done | bytes 393248 | tf_op jit(solution)/shard_map/ppermute | solution.py:21
  75.8 0.1 fusion.30
  75.9 0.1 dynamic-slice_convert_fusion.2
  76.0 0.1 collective-permute-start.2
  76.1 1.5 %collective-permute-start.3 = (bf16[4,32,512]{2,1,0:T(8,128)(2,1)S(1)}, bf16[4,32,512]{2,1,0:T(8,128)(2,1)S(1)}, u32[]{:S(2)}, u32[]{:S(2)}) collective-permute-start(bf16[4,32,512]{2,1,0:T(8,128)(2,1)S(1)} %get-tuple-element.19), channel_id=1, source_target_pairs={{0,2},{1,3},{2,0},{3,1},{4,6},{5,7},{6,4},{7,5},{8,10},{9,11},{10,... | collective-permute-start | bytes 393224 | tf_op jit(solution)/shard_map/ppermute | solution.py:15
  77.6 1.9 %collective-permute-start.4 = (bf16[4,32,512]{2,1,0:T(8,128)(2,1)S(1)}, bf16[4,32,512]{2,1,0:T(8,128)(2,1)S(1)}, u32[]{:S(2)}, u32[]{:S(2)}) collective-permute-start(bf16[4,32,512]{2,1,0:T(8,128)(2,1)S(1)} %get-tuple-element.18), channel_id=1, source_target_pairs={{0,3},{1,0},{2,1},{3,2},{4,7},{5,4},{6,5},{7,6},{8,11},{9,8},{10,9... | collective-permute-start | bytes 393224 | tf_op jit(solution)/shard_map/ppermute | solution.py:15
  79.5 2.6 %collective-permute-done.2 = bf16[4,32,512]{2,1,0:T(8,128)(2,1)S(1)} collective-permute-done((bf16[4,32,512]{2,1,0:T(8,128)(2,1)S(1)}, bf16[4,32,512]{2,1,0:T(8,128)(2,1)S(1)}, u32[]{:S(2)}, u32[]{:S(2)}) %collective-permute-start.2) | collective-permute-done | bytes 131104 | tf_op jit(solution)/shard_map/ppermute | solution.py:15
  82.1 4.8 %collective-permute-done.3 = bf16[4,32,512]{2,1,0:T(8,128)(2,1)S(1)} collective-permute-done((bf16[4,32,512]{2,1,0:T(8,128)(2,1)S(1)}, bf16[4,32,512]{2,1,0:T(8,128)(2,1)S(1)}, u32[]{:S(2)}, u32[]{:S(2)}) %collective-permute-start.3) | collective-permute-done | bytes 131104 | tf_op jit(solution)/shard_map/ppermute | solution.py:15
  87.0 2.8 %collective-permute-done.4 = bf16[4,32,512]{2,1,0:T(8,128)(2,1)S(1)} collective-permute-done((bf16[4,32,512]{2,1,0:T(8,128)(2,1)S(1)}, bf16[4,32,512]{2,1,0:T(8,128)(2,1)S(1)}, u32[]{:S(2)}, u32[]{:S(2)}) %collective-permute-start.4) | collective-permute-done | bytes 131104 | tf_op jit(solution)/shard_map/ppermute | solution.py:15
  89.8 0.8 convert_add_fusion
  (8 shorter events, 0.1 us)
Async XLA Ops:
  0.0 41.3 %copy-start = (s32[3,128]{1,0:T(4,128)S(1)}, s32[3,128]{1,0:T(4,128)}, u32[]{:S(2)}) copy-start(s32[3,128]{1,0:T(4,128)} %param.16) | copy-start | bytes 4612
  16.8 0.8 copy-start.3
  18.4 22.9 %collective-permute-start = (bf16[4,96,512]{2,1,0:T(8,128)(2,1)}, bf16[4,96,512]{2,1,0:T(8,128)(2,1)}, u32[]{:S(2)}, u32[]{:S(2)}) collective-permute-start(bf16[4,96,512]{2,1,0:T(8,128)(2,1)} %slice.61), channel_id=1, source_target_pairs={{4,0},{8,4},{12,8},{16,12},{20,16},{24,20},{28,24},{5,1},{9,5},{13... | collective-permute-start | bytes 1179656 | tf_op jit(solution)/shard_map/ppermute | solution.py:21
  37.9 2.0 %copy-start.6 = (bf16[6,3,128,128]{3,0,1,2:T(8,128)(2,1)S(1)}, bf16[6,3,128,128]{3,0,1,2:T(8,128)(2,1)}, u32[]{:S(2)}) copy-start(bf16[6,3,128,128]{3,0,1,2:T(8,128)(2,1)} %fusion.22) | copy-start | bytes 1769476
  37.9 2.1 %copy-start.5 = (bf16[6,3,128,128]{3,0,1,2:T(8,128)(2,1)S(1)}, bf16[6,3,128,128]{3,0,1,2:T(8,128)(2,1)}, u32[]{:S(2)}) copy-start(bf16[6,3,128,128]{3,0,1,2:T(8,128)(2,1)} %fusion.25) | copy-start | bytes 1769476
  39.9 0.7 copy-start.7
  39.9 0.8 copy-start.8
  39.9 1.4 %copy-start.4 = (bf16[4,128,512]{2,1,0:T(8,128)(2,1)S(1)}, bf16[4,128,512]{2,1,0:T(8,128)(2,1)}, u32[]{:S(2)}) copy-start(bf16[4,128,512]{2,1,0:T(8,128)(2,1)} %copy-done.3) | copy-start | bytes 1572868
  42.4 1.2 %copy-start.1 = (bf16[32,128,128]{2,1,0:T(8,128)(2,1)S(1)}, bf16[32,128,128]{2,1,0:T(8,128)(2,1)}, u32[]{:S(2)}) copy-start(bf16[32,128,128]{2,1,0:T(8,128)(2,1)} %ry_hbm.1) | copy-start | bytes 3145732
  43.6 1.2 %copy-start.2 = (bf16[32,128,128]{2,1,0:T(8,128)(2,1)S(1)}, bf16[32,128,128]{2,1,0:T(8,128)(2,1)}, u32[]{:S(2)}) copy-start(bf16[32,128,128]{2,1,0:T(8,128)(2,1)} %obs_hbm.1) | copy-start | bytes 3145732
  66.7 9.1 %collective-permute-start.1 = (bf16[4,96,512]{2,1,0:T(8,128)(2,1)S(1)}, bf16[4,96,512]{2,1,0:T(8,128)(2,1)S(1)}, u32[]{:S(2)}, u32[]{:S(2)}) collective-permute-start(bf16[4,96,512]{2,1,0:T(8,128)(2,1)S(1)} %slice.72), channel_id=1, source_target_pairs={{0,4},{4,8},{8,12},{12,16},{16,20},{20,24},{24,28},{1,5},{5,9},{9,... | collective-permute-start | bytes 1179656 | tf_op jit(solution)/shard_map/ppermute | solution.py:21
  76.0 6.1 %collective-permute-start.2 = (bf16[4,32,512]{2,1,0:T(8,128)(2,1)S(1)}, bf16[4,32,512]{2,1,0:T(8,128)(2,1)S(1)}, u32[]{:S(2)}, u32[]{:S(2)}) collective-permute-start(bf16[4,32,512]{2,1,0:T(8,128)(2,1)S(1)} %get-tuple-element.17), channel_id=1, source_target_pairs={{0,1},{1,2},{2,3},{3,0},{4,5},{5,6},{6,7},{7,4},{8,9},{9,10},{10,1... | collective-permute-start | bytes 393224 | tf_op jit(solution)/shard_map/ppermute | solution.py:15
  76.1 10.9 %collective-permute-start.3 = (bf16[4,32,512]{2,1,0:T(8,128)(2,1)S(1)}, bf16[4,32,512]{2,1,0:T(8,128)(2,1)S(1)}, u32[]{:S(2)}, u32[]{:S(2)}) collective-permute-start(bf16[4,32,512]{2,1,0:T(8,128)(2,1)S(1)} %get-tuple-element.19), channel_id=1, source_target_pairs={{0,2},{1,3},{2,0},{3,1},{4,6},{5,7},{6,4},{7,5},{8,10},{9,11},{10,... | collective-permute-start | bytes 393224 | tf_op jit(solution)/shard_map/ppermute | solution.py:15
  77.6 12.2 %collective-permute-start.4 = (bf16[4,32,512]{2,1,0:T(8,128)(2,1)S(1)}, bf16[4,32,512]{2,1,0:T(8,128)(2,1)S(1)}, u32[]{:S(2)}, u32[]{:S(2)}) collective-permute-start(bf16[4,32,512]{2,1,0:T(8,128)(2,1)S(1)} %get-tuple-element.18), channel_id=1, source_target_pairs={{0,3},{1,0},{2,1},{3,2},{4,7},{5,4},{6,5},{7,6},{8,11},{9,8},{10,9... | collective-permute-start | bytes 393224 | tf_op jit(solution)/shard_map/ppermute | solution.py:15

commit v2 on v1

v2 whole, which is shorter than its diff:
```python
import functools

import jax
import jax.numpy as jnp
from jax import lax
from jax.experimental import pallas as pl
from jax.experimental.pallas import tpu as pltpu
from jax.sharding import PartitionSpec as P

GROUPS = (8, 4, 2)
ROW_ALIGN = 32
VMEM_LIMIT = 16 * 1024 * 1024
SMALL_VMEM_LIMIT = 4 * 1024 * 1024


def shifted(block, axis, distance):
    size = lax.axis_size(axis)
    return lax.ppermute(block, axis, [(i, (i + distance) % size) for i in range(size)])


def passed_along(block, axis, distance):
    devices = range(lax.axis_size(axis))
    route = [(i - distance, i) for i in devices if i - distance in devices]
    return lax.ppermute(block, axis, route)


def dot(a, b, contract):
    return lax.dot_general(a, b, ((contract[:1], contract[1:]), ((), ())), preferred_element_type=jnp.float32)


def prepare_kernel(
    tile_rows,
    taps_hbm,
    sed_hbm,
    meta_hbm,
    counts_hbm,
    ry_hbm,
    rx_hbm,
    obs_hbm,
    py_ref,
    py_t_ref,
    px_ref,
    px_t_ref,
    ry_ref,
    rx_ref,
    obs_ref,
    sed_ref,
    *rest,
):
    plans, (taps_ref, lines_ref, meta_ref, counts_ref, sems) = rest[:-5], rest[-5:]
    bands, terms, axes, tap_count = taps_ref.shape
    slots = ry_ref.shape[0]
    half = tap_count // 2
    moves = [
        pltpu.make_async_copy(source, target, sems.at[i])
        for i, (source, target) in enumerate(
            (
                (taps_hbm, taps_ref),
                (meta_hbm, meta_ref),
                (counts_hbm, counts_ref),
                (sed_hbm, sed_ref),
                (ry_hbm, ry_ref),
                (rx_hbm, rx_ref),
                (obs_hbm, obs_ref),
            )
        )
    ]
    for move in moves:
        move.start()
    lines_ref[...] = jnp.zeros_like(lines_ref)
    lanes = lines_ref.shape[2]
    mirror = lax.broadcasted_iota(jnp.int32, (lanes, lanes), 0) + lax.broadcasted_iota(jnp.int32, (lanes, lanes), 1)
    mirror = (mirror == tap_count - 1).astype(jnp.bfloat16)
    for move in moves[:3]:
        move.wait()

    def one_band(b, carry):
        for t in range(terms):
            lines_ref[b, axes * t : axes * (t + 1), :tap_count] = taps_ref[b, t]
        forward = lines_ref[b].astype(jnp.bfloat16)
        mirrored = dot(forward, mirror, (1, 0))
        forward = forward.astype(jnp.float32)
        for axis, (turned_ref, straight_ref) in enumerate(((py_ref, py_t_ref), (px_ref, px_t_ref))):
            width = straight_ref.shape[1]
            down = lax.broadcasted_iota(jnp.int32, (width, width), 0)
            right = lax.broadcasted_iota(jnp.int32, (width, width), 1)
            near = jnp.abs(down - right) <= half
            for lines, out_ref in ((forward, straight_ref), (mirrored, turned_ref)):
                if width > lanes:
                    lines = jnp.concatenate([lines, jnp.zeros((lines.shape[0], width - lanes), jnp.float32)], axis=1)
                centred = pltpu.roll(lines, width - half, 1)
                for t in range(terms):
                    line = centred[axes * t + axis : axes * t + axis + 1]
                    rolled = pltpu.roll(jnp.broadcast_to(line, (width, width)), 0, 1, stride=1, stride_axis=0)
                    table = jnp.where(near, rolled, 0.0)
                    out_ref[b, :, t * width : (t + 1) * width] = table.astype(jnp.bfloat16)
        return carry

    lax.fori_loop(0, bands, one_band, 0, unroll=True)

    mine = lax.axis_index("shard")

    def place(slot, found):
        at = mine * slots + slot
        col = meta_ref[1, at]
        after = []
        for c, plan_ref in enumerate(plans):
            hit = col == c
            plan_ref[1 + found[c]] = slot
            plan_ref[1 + slots + found[c]] = meta_ref[0, at] * tile_rows
            plan_ref[1 + 2 * slots + found[c]] = meta_ref[2, at]
            after.append(found[c] + hit.astype(jnp.int32))
        return tuple(after)

    found = lax.fori_loop(0, counts_ref[0, mine], place, (jnp.int32(0),) * len(plans))
    for plan_ref, total in zip(plans, found):
        plan_ref[0] = total
    for move in moves[3:]:
        move.wait()


def gather_kernel(*refs):
    tiles, (_, whole_ref, rim_ref) = refs[:-3], refs[-3:]
    count = len(tiles)
    tile_rows = tiles[0].shape[1]
    rim_tiles = rim_ref.shape[1] // tile_rows
    for k in range(count):
        owner = lax.rem(lax.axis_index("shard") + (count - k), count)
        place = pl.ds(pl.multiple_of(owner * tile_rows, tile_rows), tile_rows)
        whole_ref[:, place, :] = tiles[k][...]

        @pl.when(owner < rim_tiles)
        def _(place=place, tile=tiles[k]):
            rim_ref[:, place, :] = tile[...]


def exposures_kernel(
    terms,
    plan_ref,
    sed_ref,
    whole_ref,
    next_ref,
    py_ref,
    py_t_ref,
    px_ref,
    px_t_ref,
    ry_ref,
    rx_ref,
    obs_ref,
    own_ref,
    spill_ref,
    mix_ref,
    acc_ref,
):
    channels, bands = sed_ref.shape
    region_rows = whole_ref.shape[1]
    rim_rows = next_ref.shape[1]
    slots, _, win_rows = ry_ref.shape
    win_cols = rx_ref.shape[2]
    count = plan_ref[0]
    acc_ref[...] = jnp.zeros_like(acc_ref)

    def mix(b, carry):
        for part_ref, start in ((whole_ref, 0), (next_ref, region_rows)):
            total = None
            for k in range(channels):
                term = sed_ref[k, b] * part_ref[k].astype(jnp.float32)
                total = term if total is None else total + term
            mix_ref[b, start : start + part_ref.shape[1], :] = total.astype(jnp.bfloat16)
        return carry

    lax.fori_loop(0, bands, mix, 0)

    def visit(group, first):
        members = range(group)
        live = [first + m < count for m in members]
        rank = [jnp.minimum(first + m, count - 1) for m in members]
        slot_of = [plan_ref[1 + r] for r in rank]
        row = [pl.multiple_of(plan_ref[1 + slots + r], ROW_ALIGN) for r in rank]
        band = [plan_ref[1 + 2 * slots + r] for r in rank]
        mixed = [mix_ref[band[m], pl.ds(row[m], win_rows), :] for m in members]
        along = [dot(mixed[m], px_t_ref[band[m]], (1, 0)).astype(jnp.bfloat16) for m in members]
        stack = [
            jnp.concatenate([along[m][:, t * win_cols : (t + 1) * win_cols] for t in range(terms)], axis=0)
            for m in members
        ]
        blurred = [dot(py_ref[band[m]], stack[m], (1, 0)).astype(jnp.bfloat16) for m in members]
        sampled = [dot(ry_ref[slot_of[m]], blurred[m], (1, 0)).astype(jnp.bfloat16) for m in members]
        model = [dot(sampled[m], rx_ref[slot_of[m]], (1, 1)) for m in members]
        misfit = [(model[m] - obs_ref[slot_of[m]].astype(jnp.float32)).astype(jnp.bfloat16) for m in members]
        back_rows = [dot(ry_ref[slot_of[m]], misfit[m], (0, 0)).astype(jnp.bfloat16) for m in members]
        back = [dot(back_rows[m], rx_ref[slot_of[m]], (1, 0)).astype(jnp.bfloat16) for m in members]
        spread = [dot(back[m], px_ref[band[m]], (1, 0)).astype(jnp.bfloat16) for m in members]
        back_along = [
            jnp.concatenate([spread[m][:, t * win_cols : (t + 1) * win_cols] for t in range(terms)], axis=0)
            for m in members
        ]
        window_grad = [dot(py_t_ref[band[m]], back_along[m], (1, 0)) for m in members]
        for m in members:
            place = (band[m], pl.ds(row[m], win_rows), slice(None))
            acc_ref[place] = acc_ref[place] + jnp.where(live[m], window_grad[m], 0.0)

    done = jnp.int32(0)
    for at, group in enumerate(GROUPS):
        left = count - done
        turns = left // group if at < len(GROUPS) - 1 else (left + group - 1) // group

        def turn(i, carry, group=group, done=done):
            visit(group, done + i * group)
            return carry

        lax.fori_loop(0, turns, turn, 0)
        done = done + turns * group

    for k in range(channels):
        for out_ref, start, rows in ((spill_ref, region_rows, rim_rows), (own_ref, 0, region_rows)):
            total = None
            for b in range(bands):
                term = sed_ref[k, b] * acc_ref[b, start : start + rows, :]
                total = term if total is None else total + term
            out_ref[k] = total.astype(out_ref.dtype)


def share_kernel(own_ref, spilled_ref, kept_ref, *given):
    count = 1 + len(given)
    tile_rows = kept_ref.shape[1]
    rim_tiles = spilled_ref.shape[1] // tile_rows
    for k, out_ref in enumerate((kept_ref,) + given):
        owner = lax.rem(lax.axis_index("shard") + k, count)
        tile = own_ref[:, pl.ds(pl.multiple_of(owner * tile_rows, tile_rows), tile_rows), :]
        rim = pl.ds(pl.multiple_of(jnp.minimum(owner, rim_tiles - 1) * tile_rows, tile_rows), tile_rows)
        extra = jnp.where(owner < rim_tiles, spilled_ref[:, rim, :].astype(jnp.float32), 0.0)
        out_ref[...] = (tile + extra).astype(out_ref.dtype)


def local(
    planes,
    sed_weights,
    psf_taps,
    resample_rows,
    resample_cols,
    observed,
    exposure_meta,
    slot_counts,
):
    shard_count = lax.axis_size("shard")
    channel_count, tile_rows, col_total = planes.shape
    slot_count, out_rows, win_rows = resample_rows.shape
    win_cols = resample_cols.shape[2]
    col_tiles = col_total // win_cols
    region_rows = tile_rows * shard_count
    rim_rows = win_rows - tile_rows
    bands, terms, tap_count = psf_taps.shape[1:]
    smem = pl.BlockSpec(memory_space=pltpu.SMEM)
    vmem = pl.BlockSpec(memory_space=pltpu.VMEM)
    anywhere = pl.BlockSpec(memory_space=pl.ANY)
    tile_shape = (channel_count, tile_rows, win_cols)
    whole_shape = (channel_count, region_rows, win_cols)
    rim_shape = (channel_count, rim_rows, win_cols)

    tiles = []
    for c in range(col_tiles):
        own = planes[:, :, c * win_cols : (c + 1) * win_cols]
        tiles.append([own] + [shifted(own, "shard", k) for k in range(1, shard_count)])

    def spec(*shape):
        return jax.ShapeDtypeStruct(shape, jnp.bfloat16)

    prepared = pl.pallas_call(
        functools.partial(prepare_kernel, tile_rows),
        out_shape=(
            spec(bands, win_rows, terms * win_rows),
            spec(bands, win_rows, terms * win_rows),
            spec(bands, win_cols, terms * win_cols),
            spec(bands, win_cols, terms * win_cols),
            spec(*resample_rows.shape),
            spec(*resample_cols.shape),
            spec(*observed.shape),
            jax.ShapeDtypeStruct(sed_weights.shape[::-1], jnp.float32),
        )
        + (jax.ShapeDtypeStruct((1 + 3 * slot_count,), jnp.int32),) * col_tiles,
        in_specs=[anywhere] * 7,
        out_specs=(vmem,) * 7 + (smem,) * (1 + col_tiles),
        scratch_shapes=[
            pltpu.VMEM((bands, terms, 2, tap_count), jnp.float32),
            pltpu.VMEM((bands, 8 * ((2 * terms + 7) // 8), 128), jnp.float32),
            pltpu.SMEM(exposure_meta.shape, jnp.int32),
            pltpu.SMEM(slot_counts.shape, jnp.int32),
            pltpu.SemaphoreType.DMA((7,)),
        ],
        compiler_params=pltpu.CompilerParams(vmem_limit_bytes=VMEM_LIMIT),
        cost_estimate=pl.CostEstimate(flops=10**8, bytes_accessed=4 * 10**6, transcendentals=0),
    )(
        *(
            pltpu.with_memory_space_constraint(x, pltpu.HBM)
            for x in (
                psf_taps.transpose(1, 2, 0, 3),
                sed_weights.T,
                exposure_meta,
                slot_counts,
                resample_rows,
                resample_cols,
                observed,
            )
        )
    )
    plans = prepared[8:]

    result = []
    after = prepared[0]
    for c in range(col_tiles):
        whole, rim = pl.pallas_call(
            gather_kernel,
            out_shape=(
                jax.ShapeDtypeStruct(whole_shape, planes.dtype),
                jax.ShapeDtypeStruct(rim_shape, planes.dtype),
            ),
            in_specs=[vmem] * shard_count + [anywhere],
            out_specs=(vmem, vmem),
            compiler_params=pltpu.CompilerParams(vmem_limit_bytes=SMALL_VMEM_LIMIT),
            cost_estimate=pl.CostEstimate(flops=10**5, bytes_accessed=10**6, transcendentals=0),
        )(*tiles[c], after)
        following = passed_along(rim, "region", -1)
        own_rows, spill = pl.pallas_call(
            functools.partial(exposures_kernel, terms),
            out_shape=(
                jax.ShapeDtypeStruct(whole_shape, jnp.float32),
                jax.ShapeDtypeStruct(rim_shape, jnp.bfloat16),
            ),
            in_specs=[smem] * 2 + [vmem] * 9,
            out_specs=(vmem, vmem),
            scratch_shapes=[
                pltpu.VMEM((bands, region_rows + rim_rows, win_cols), jnp.bfloat16),
                pltpu.VMEM((bands, region_rows + rim_rows, win_cols), jnp.float32),
            ],
            compiler_params=pltpu.CompilerParams(vmem_limit_bytes=VMEM_LIMIT),
            cost_estimate=pl.CostEstimate(flops=6 * 10**9, bytes_accessed=6 * 10**6, transcendentals=0),
        )(plans[c], prepared[7], whole, following, *prepared[:7])
        after = own_rows
        spilled = passed_along(spill, "region", 1)
        total, *given = pl.pallas_call(
            share_kernel,
            out_shape=(jax.ShapeDtypeStruct(tile_shape, jnp.float32),)
            + (jax.ShapeDtypeStruct(tile_shape, jnp.bfloat16),) * (shard_count - 1),
            in_specs=[vmem] * 2,
            out_specs=(vmem,) * shard_count,
            compiler_params=pltpu.CompilerParams(vmem_limit_bytes=SMALL_VMEM_LIMIT),
            cost_estimate=pl.CostEstimate(flops=10**5, bytes_accessed=10**6, transcendentals=0),
        )(own_rows, spilled)
        for step in range(1, shard_count):
            total = total + shifted(given[step - 1], "shard", step).astype(jnp.float32)
        result.append(total)
    return jnp.concatenate(result, axis=2)


def solution(mesh):
    placed = (
        P(None, ("region", "shard"), None),
        P(),
        P(),
        P(("region", "shard"), None, None),
        P(("region", "shard"), None, None),
        P(("region", "shard"), None, None),
        P(None, "region"),
        P("region", None),
    )
    return jax.shard_map(
        local,
        mesh=mesh,
        in_specs=placed,
        out_specs=P(None, ("region", "shard"), None),
        check_vma=False,
    )
```

time: 90.5 us -> 59.8 us (0.66); the launches traced: 90.6 us -> 58.7 us
  starting transfers between devices: 7.34 us -> 35.2 us
  blocking collectives: 16.8 us -> 0 us
  matrix products: 12.6 us -> 0 us
  local copies, waits for them, and re-layouts: 12.5 us -> 0.88 us
  Pallas kernels: 21.8 us -> 12.7 us
  waiting for transfers between devices: 17.3 us -> 8.85 us
  other arithmetic: 1.97 us -> 0.8 us
    ppermute x3 -> x12, starting transfers between devices: 3.51 us -> 24.6 us  [shifted(): lax.ppermute(block, axis, [(i, (i + distance) % size) for i in range(size)])]
    all_gather x1 -> x0, blocking collectives: 16.8 us -> none  [local(): gathered = lax.all_gather(planes, 'shard', axis=1, tiled=True)]
    dot_general x4 -> x0, matrix products: 12.6 us -> none  [band_tables(): jnp.einsum('btk,kij->btij', taps, selector, precision=lax.Precision.HIGHEST)]
    pallas_call x1 -> x7, Pallas kernels: 21.8 us -> 12.7 us  [the longest x2 8.87 us: local(): pl.pallas_call(functools.partial(exposures_kernel, terms), out_shape=(jax...]
    ppermute x2 -> x4, starting transfers between devices: 3.83 us -> 10.6 us  [passed_along(): return lax.ppermute(block, axis, route)]
    ppermute x2 -> x4, waiting for transfers between devices: 7.05 us -> 0.76 us  [passed_along(): return lax.ppermute(block, axis, route)]
    convert_element_type x5 -> x0, local copies, waits for them, and re-layouts: 6.12 us -> none  [the longest x4 6.06 us: band_tables(): return table.astype(jnp.bfloat16).reshape(bands, terms * width, width)]
    unnamed x21 -> x0, local copies, waits for them, and re-layouts: 3.77 us -> none
  transfers between devices with their start and end apart: 5 -> 16, of which waited for: 4 -> 5; matrix products, arithmetic and copies ran while one was open for 23% -> 0% of each run, Pallas kernels for 0% -> 22%
where the time goes in v2:
time: 59.8 us; the launch traced here: 58.7 us
  starting transfers between devices  35.2 us (59%)
  Pallas kernels  12.7 us (21%)
  waiting for transfers between devices  8.85 us (15%)
  local copies, waits for them, and re-layouts  0.88 us (1%)
  other arithmetic  0.8 us (1%)
    ppermute x12, starting transfers between devices, shifted(): lax.ppermute(block, axis, [(i, (i + distance) % size) for i in range(size)])  24.6 us
    ppermute x4, starting transfers between devices, passed_along(): return lax.ppermute(block, axis, route)  10.6 us
    pallas_call x2, Pallas kernels, local(): pl.pallas_call(functools.partial(exposures_kernel, terms), out_shape=(jax...  8.87 us
    ppermute x12, waiting for transfers between devices, shifted(): lax.ppermute(block, axis, [(i, (i + distance) % size) for i in range(size)])  8.09 us
    pallas_call x1, Pallas kernels, local(): pl.pallas_call(functools.partial(prepare_kernel, tile_rows), out_shape=(s...  3.63 us
  transfers between devices with their start and end apart: 16, of which 5 were waited for; matrix products, arithmetic and copies ran while one was open for 0% of the time, Pallas kernels for 22%

profile of v2, /device:TPU:10, one launch (start us, length us, event | category | flops | bytes accessed | tf_op | source)
XLA Modules:
  0.0 58.7 jit_solution(7237784067565641741)
XLA Ops:
  0.0 0.9 %fusion = (bf16[4,32,256]{2,1,0:T(8,128)(2,1)S(1)}, bf16[4,32,256]{2,1,0:T(8,128)(2,1)S(1)}) fusion(bf16[4,32,512]{2,1,0:T(8,128)(2,1)} %param.8), kind=kLoop, calls=%fused_computation.3 | loop fusion | bytes 262144 | tf_op jit(solution)/shard_map/slice | solution.py:263
  0.9 1.6 %collective-permute-start = (bf16[4,32,256]{2,1,0:T(8,128)(2,1)S(1)}, bf16[4,32,256]{2,1,0:T(8,128)(2,1)S(1)}, u32[]{:S(2)}, u32[]{:S(2)}) collective-permute-start(bf16[4,32,256]{2,1,0:T(8,128)(2,1)S(1)} %get-tuple-element.57.refs_0_), channel_id=1, source_target_pairs={{0,1},{1,2},{2,3},{3,0},{4,5},{5,6},{6,7},{7,4},{8,9},{9,10},{10,1... | collective-permute-start | bytes 196616 | tf_op jit(solution)/shard_map/ppermute | solution.py:18
  2.5 1.2 %collective-permute-start.1 = (bf16[4,32,256]{2,1,0:T(8,128)(2,1)S(1)}, bf16[4,32,256]{2,1,0:T(8,128)(2,1)S(1)}, u32[]{:S(2)}, u32[]{:S(2)}) collective-permute-start(bf16[4,32,256]{2,1,0:T(8,128)(2,1)S(1)} %get-tuple-element.57.refs_0_), channel_id=1, source_target_pairs={{0,2},{1,3},{2,0},{3,1},{4,6},{5,7},{6,4},{7,5},{8,10},{9,11},{10,... | collective-permute-start | bytes 196616 | tf_op jit(solution)/shard_map/ppermute | solution.py:18
  3.7 1.8 %collective-permute-start.2 = (bf16[4,32,256]{2,1,0:T(8,128)(2,1)S(1)}, bf16[4,32,256]{2,1,0:T(8,128)(2,1)S(1)}, u32[]{:S(2)}, u32[]{:S(2)}) collective-permute-start(bf16[4,32,256]{2,1,0:T(8,128)(2,1)S(1)} %get-tuple-element.57.refs_0_), channel_id=1, source_target_pairs={{0,3},{1,0},{2,1},{3,2},{4,7},{5,4},{6,5},{7,6},{8,11},{9,8},{10,9... | collective-permute-start | bytes 196616 | tf_op jit(solution)/shard_map/ppermute | solution.py:18
  5.6 3.6 %shard_map.82 = (bf16[6,128,384]{2,1,0:T(8,128)(2,1)S(1)}, bf16[6,128,384]{2,1,0:T(8,128)(2,1)S(1)}, bf16[6,256,768]{2,1,0:T(8,128)(2,1)S(1)}, bf16[6,256,768]{2...) custom-call(f32[6,3,2,25]{3,2,1,0:T(2,128)} %bitcast.2, ...), custom_call_target="tpu_custom_call" | custom-call | flops 100000000 | bytes 4000000 | tf_op jit(solution)/shard_map/pallas_call | solution.py:269
  9.2 0.0 collective-permute-done.refs_1_
  9.2 0.0 collective-permute-done.1.refs_2_
  9.2 0.6 %collective-permute-done.2.refs_3_ = bf16[4,32,256]{2,1,0:T(8,128)(2,1)S(1)} collective-permute-done((bf16[4,32,256]{2,1,0:T(8,128)(2,1)S(1)}, bf16[4,32,256]{2,1,0:T(8,128)(2,1)S(1)}, u32[]{:S(2)}, u32[]{:S(2)}) %collective-permute-start.2) | collective-permute-done | bytes 65568 | tf_op jit(solution)/shard_map/ppermute | solution.py:18
  9.9 2.0 %collective-permute-start.3 = (bf16[4,96,256]{2,1,0:T(8,128)(2,1)S(1)}, bf16[4,96,256]{2,1,0:T(8,128)(2,1)S(1)}, u32[]{:S(2)}, u32[]{:S(2)}) collective-permute-start(bf16[4,96,256]{2,1,0:T(8,128)(2,1)S(1)} %get-tuple-element.35), channel_id=1, source_target_pairs={{4,0},{8,4},{12,8},{16,12},{20,16},{24,20},{28,24},{5,1},{9,5},{13... | collective-permute-start | bytes 589832 | tf_op jit(solution)/shard_map/ppermute | solution.py:24
  11.9 0.8 %collective-permute-start.10 = (bf16[4,32,256]{2,1,0:T(8,128)(2,1)S(1)}, bf16[4,32,256]{2,1,0:T(8,128)(2,1)S(1)}, u32[]{:S(2)}, u32[]{:S(2)}) collective-permute-start(bf16[4,32,256]{2,1,0:T(8,128)(2,1)S(1)} %get-tuple-element.58.refs_0_), channel_id=1, source_target_pairs={{0,3},{1,0},{2,1},{3,2},{4,7},{5,4},{6,5},{7,6},{8,11},{9,8},{10,9... | collective-permute-start | bytes 196616 | tf_op jit(solution)/shard_map/ppermute | solution.py:18
  12.7 1.3 %collective-permute-start.8 = (bf16[4,32,256]{2,1,0:T(8,128)(2,1)S(1)}, bf16[4,32,256]{2,1,0:T(8,128)(2,1)S(1)}, u32[]{:S(2)}, u32[]{:S(2)}) collective-permute-start(bf16[4,32,256]{2,1,0:T(8,128)(2,1)S(1)} %get-tuple-element.58.refs_0_), channel_id=1, source_target_pairs={{0,1},{1,2},{2,3},{3,0},{4,5},{5,6},{6,7},{7,4},{8,9},{9,10},{10,1... | collective-permute-start | bytes 196616 | tf_op jit(solution)/shard_map/ppermute | solution.py:18
  14.0 3.7 %collective-permute-start.9 = (bf16[4,32,256]{2,1,0:T(8,128)(2,1)S(1)}, bf16[4,32,256]{2,1,0:T(8,128)(2,1)S(1)}, u32[]{:S(2)}, u32[]{:S(2)}) collective-permute-start(bf16[4,32,256]{2,1,0:T(8,128)(2,1)S(1)} %get-tuple-element.58.refs_0_), channel_id=1, source_target_pairs={{0,2},{1,3},{2,0},{3,1},{4,6},{5,7},{6,4},{7,5},{8,10},{9,11},{10,... | collective-permute-start | bytes 196616 | tf_op jit(solution)/shard_map/ppermute | solution.py:18
  17.7 0.0 collective-permute-done.3.next_ref
  17.7 4.4 %shard_map.84 = (f32[4,128,256]{2,1,0:T(8,128)S(1)}, bf16[4,96,256]{2,1,0:T(8,128)(2,1)S(1)}) custom-call(s32[97]{0:T(128)S(1)} %get-tuple-element.31.plan_ref, f32[4,6]{1,0:T(4,128)S(1)} %get-tuple-element.32.sed_ref, bf16[4,128,256]{2,1,0:T(8,128)(2,1)S(1)} %get-tuple-element.34.whole_ref, bf16[4,96,256]{2,1,0:T(8,128)(2,1)S(1)} %collective-permute-done.3.next_ref, ...), custom_call_target="tpu_custom_call" | custom-call | flops 6000000000 | bytes 6000000 | tf_op jit(solution)/shard_map/pallas_call | solution.py:324
  22.2 0.0 collective-permute-done.10.refs_3_
  22.2 0.0 collective-permute-done.8.refs_1_
  22.2 0.0 collective-permute-done.9.refs_2_
  22.2 0.1 shard_map.86
  22.3 1.9 %collective-permute-start.11 = (bf16[4,96,256]{2,1,0:T(8,128)(2,1)S(1)}, bf16[4,96,256]{2,1,0:T(8,128)(2,1)S(1)}, u32[]{:S(2)}, u32[]{:S(2)}) collective-permute-start(bf16[4,96,256]{2,1,0:T(8,128)(2,1)S(1)} %get-tuple-element.50), channel_id=1, source_target_pairs={{4,0},{8,4},{12,8},{16,12},{20,16},{24,20},{28,24},{5,1},{9,5},{13... | collective-permute-start | bytes 589832 | tf_op jit(solution)/shard_map/ppermute | solution.py:24
  24.2 2.4 %collective-permute-start.4 = (bf16[4,96,256]{2,1,0:T(8,128)(2,1)S(1)}, bf16[4,96,256]{2,1,0:T(8,128)(2,1)S(1)}, u32[]{:S(2)}, u32[]{:S(2)}) collective-permute-start(bf16[4,96,256]{2,1,0:T(8,128)(2,1)S(1)} %get-tuple-element.43), channel_id=1, source_target_pairs={{0,4},{4,8},{8,12},{12,16},{16,20},{20,24},{24,28},{1,5},{5,9},{9,... | collective-permute-start | bytes 589832 | tf_op jit(solution)/shard_map/ppermute | solution.py:24
  26.6 0.8 %collective-permute-done.11.next_ref = bf16[4,96,256]{2,1,0:T(8,128)(2,1)S(1)} collective-permute-done((bf16[4,96,256]{2,1,0:T(8,128)(2,1)S(1)}, bf16[4,96,256]{2,1,0:T(8,128)(2,1)S(1)}, u32[]{:S(2)}, u32[]{:S(2)}) %collective-permute-start.11) | collective-permute-done | bytes 196640 | tf_op jit(solution)/shard_map/ppermute | solution.py:24
  27.3 4.4 %shard_map.87 = (f32[4,128,256]{2,1,0:T(8,128)S(1)}, bf16[4,96,256]{2,1,0:T(8,128)(2,1)S(1)}) custom-call(s32[97]{0:T(128)S(1)} %get-tuple-element.48.plan_ref, f32[4,6]{1,0:T(4,128)S(1)} %get-tuple-element.32.sed_ref, bf16[4,128,256]{2,1,0:T(8,128)(2,1)S(1)} %get-tuple-element.49.whole_ref, bf16[4,96,256]{2,1,0:T(8,128)(2,1)S(1)} %collective-permute-done.11.next_ref, ...), custom_call_target="tpu_custom_call" | custom-call | flops 6000000000 | bytes 6000000 | tf_op jit(solution)/shard_map/pallas_call | solution.py:324
  31.8 4.3 %collective-permute-start.12 = (bf16[4,96,256]{2,1,0:T(8,128)(2,1)S(1)}, bf16[4,96,256]{2,1,0:T(8,128)(2,1)S(1)}, u32[]{:S(2)}, u32[]{:S(2)}) collective-permute-start(bf16[4,96,256]{2,1,0:T(8,128)(2,1)S(1)} %get-tuple-element.52), channel_id=1, source_target_pairs={{0,4},{4,8},{8,12},{12,16},{16,20},{20,24},{24,28},{1,5},{5,9},{9,... | collective-permute-start | bytes 589832 | tf_op jit(solution)/shard_map/ppermute | solution.py:24
  36.1 0.0 collective-permute-done.4.spilled_ref
  36.1 0.1 shard_map.85
  36.2 0.5 collective-permute-start.5
  36.7 9.8 %collective-permute-start.6 = (bf16[4,32,256]{2,1,0:T(8,128)(2,1)S(1)}, bf16[4,32,256]{2,1,0:T(8,128)(2,1)S(1)}, u32[]{:S(2)}, u32[]{:S(2)}) collective-permute-start(bf16[4,32,256]{2,1,0:T(8,128)(2,1)S(1)} %get-tuple-element.46), channel_id=1, source_target_pairs={{0,2},{1,3},{2,0},{3,1},{4,6},{5,7},{6,4},{7,5},{8,10},{9,11},{10,... | collective-permute-start | bytes 196616 | tf_op jit(solution)/shard_map/ppermute | solution.py:18
  46.4 0.0 collective-permute-start.7
  46.4 0.0 collective-permute-done.12.spilled_ref
  46.4 0.1 shard_map.88
  46.5 2.1 %collective-permute-start.13 = (bf16[4,32,256]{2,1,0:T(8,128)(2,1)S(1)}, bf16[4,32,256]{2,1,0:T(8,128)(2,1)S(1)}, u32[]{:S(2)}, u32[]{:S(2)}) collective-permute-start(bf16[4,32,256]{2,1,0:T(8,128)(2,1)S(1)} %get-tuple-element.54), channel_id=1, source_target_pairs={{0,1},{1,2},{2,3},{3,0},{4,5},{5,6},{6,7},{7,4},{8,9},{9,10},{10,1... | collective-permute-start | bytes 196616 | tf_op jit(solution)/shard_map/ppermute | solution.py:18
  48.6 1.8 %collective-permute-start.14 = (bf16[4,32,256]{2,1,0:T(8,128)(2,1)S(1)}, bf16[4,32,256]{2,1,0:T(8,128)(2,1)S(1)}, u32[]{:S(2)}, u32[]{:S(2)}) collective-permute-start(bf16[4,32,256]{2,1,0:T(8,128)(2,1)S(1)} %get-tuple-element.55), channel_id=1, source_target_pairs={{0,2},{1,3},{2,0},{3,1},{4,6},{5,7},{6,4},{7,5},{8,10},{9,11},{10,... | collective-permute-start | bytes 196616 | tf_op jit(solution)/shard_map/ppermute | solution.py:18
  50.4 0.0 collective-permute-done.5
  50.4 0.0 collective-permute-start.15
  50.4 0.0 collective-permute-done.6
  50.4 2.1 %collective-permute-done.7 = bf16[4,32,256]{2,1,0:T(8,128)(2,1)S(1)} collective-permute-done((bf16[4,32,256]{2,1,0:T(8,128)(2,1)S(1)}, bf16[4,32,256]{2,1,0:T(8,128)(2,1)S(1)}, u32[]{:S(2)}, u32[]{:S(2)}) %collective-permute-start.7) | collective-permute-done | bytes 65568 | tf_op jit(solution)/shard_map/ppermute | solution.py:18
  52.6 0.0 collective-permute-done.13
  52.6 3.2 %collective-permute-done.14 = bf16[4,32,256]{2,1,0:T(8,128)(2,1)S(1)} collective-permute-done((bf16[4,32,256]{2,1,0:T(8,128)(2,1)S(1)}, bf16[4,32,256]{2,1,0:T(8,128)(2,1)S(1)}, u32[]{:S(2)}, u32[]{:S(2)}) %collective-permute-start.14) | collective-permute-done | bytes 65568 | tf_op jit(solution)/shard_map/ppermute | solution.py:18
  55.7 2.2 %collective-permute-done.15 = bf16[4,32,256]{2,1,0:T(8,128)(2,1)S(1)} collective-permute-done((bf16[4,32,256]{2,1,0:T(8,128)(2,1)S(1)}, bf16[4,32,256]{2,1,0:T(8,128)(2,1)S(1)}, u32[]{:S(2)}, u32[]{:S(2)}) %collective-permute-start.15) | collective-permute-done | bytes 65568 | tf_op jit(solution)/shard_map/ppermute | solution.py:18
  57.9 0.7 %pad_maximum_fusion = f32[4,32,512]{2,1,0:T(8,128)} fusion(f32[4,32,256]{2,1,0:T(8,128)S(1)} %convert_add_fusion, f32[4,32,256]{2,1,0:T(8,128)S(1)} %convert_add_fusion.1), kind=kLoop, calls=%fused_computation | loop fusion | flops 65536 | bytes 524288 | tf_op jit(solution)/shard_map/concatenate | solution.py:353
  (3 shorter events, 0.1 us)
Async XLA Ops:
  0.9 8.3 %collective-permute-start = (bf16[4,32,256]{2,1,0:T(8,128)(2,1)S(1)}, bf16[4,32,256]{2,1,0:T(8,128)(2,1)S(1)}, u32[]{:S(2)}, u32[]{:S(2)}) collective-permute-start(bf16[4,32,256]{2,1,0:T(8,128)(2,1)S(1)} %get-tuple-element.57.refs_0_), channel_id=1, source_target_pairs={{0,1},{1,2},{2,3},{3,0},{4,5},{5,6},{6,7},{7,4},{8,9},{9,10},{10,1... | collective-permute-start | bytes 196616 | tf_op jit(solution)/shard_map/ppermute | solution.py:18
  2.5 6.7 %collective-permute-start.1 = (bf16[4,32,256]{2,1,0:T(8,128)(2,1)S(1)}, bf16[4,32,256]{2,1,0:T(8,128)(2,1)S(1)}, u32[]{:S(2)}, u32[]{:S(2)}) collective-permute-start(bf16[4,32,256]{2,1,0:T(8,128)(2,1)S(1)} %get-tuple-element.57.refs_0_), channel_id=1, source_target_pairs={{0,2},{1,3},{2,0},{3,1},{4,6},{5,7},{6,4},{7,5},{8,10},{9,11},{10,... | collective-permute-start | bytes 196616 | tf_op jit(solution)/shard_map/ppermute | solution.py:18
  3.7 6.1 %collective-permute-start.2 = (bf16[4,32,256]{2,1,0:T(8,128)(2,1)S(1)}, bf16[4,32,256]{2,1,0:T(8,128)(2,1)S(1)}, u32[]{:S(2)}, u32[]{:S(2)}) collective-permute-start(bf16[4,32,256]{2,1,0:T(8,128)(2,1)S(1)} %get-tuple-element.57.refs_0_), channel_id=1, source_target_pairs={{0,3},{1,0},{2,1},{3,2},{4,7},{5,4},{6,5},{7,6},{8,11},{9,8},{10,9... | collective-permute-start | bytes 196616 | tf_op jit(solution)/shard_map/ppermute | solution.py:18
  9.9 7.8 %collective-permute-start.3 = (bf16[4,96,256]{2,1,0:T(8,128)(2,1)S(1)}, bf16[4,96,256]{2,1,0:T(8,128)(2,1)S(1)}, u32[]{:S(2)}, u32[]{:S(2)}) collective-permute-start(bf16[4,96,256]{2,1,0:T(8,128)(2,1)S(1)} %get-tuple-element.35), channel_id=1, source_target_pairs={{4,0},{8,4},{12,8},{16,12},{20,16},{24,20},{28,24},{5,1},{9,5},{13... | collective-permute-start | bytes 589832 | tf_op jit(solution)/shard_map/ppermute | solution.py:24
  11.9 10.3 %collective-permute-start.10 = (bf16[4,32,256]{2,1,0:T(8,128)(2,1)S(1)}, bf16[4,32,256]{2,1,0:T(8,128)(2,1)S(1)}, u32[]{:S(2)}, u32[]{:S(2)}) collective-permute-start(bf16[4,32,256]{2,1,0:T(8,128)(2,1)S(1)} %get-tuple-element.58.refs_0_), channel_id=1, source_target_pairs={{0,3},{1,0},{2,1},{3,2},{4,7},{5,4},{6,5},{7,6},{8,11},{9,8},{10,9... | collective-permute-start | bytes 196616 | tf_op jit(solution)/shard_map/ppermute | solution.py:18
  12.7 9.5 %collective-permute-start.8 = (bf16[4,32,256]{2,1,0:T(8,128)(2,1)S(1)}, bf16[4,32,256]{2,1,0:T(8,128)(2,1)S(1)}, u32[]{:S(2)}, u32[]{:S(2)}) collective-permute-start(bf16[4,32,256]{2,1,0:T(8,128)(2,1)S(1)} %get-tuple-element.58.refs_0_), channel_id=1, source_target_pairs={{0,1},{1,2},{2,3},{3,0},{4,5},{5,6},{6,7},{7,4},{8,9},{9,10},{10,1... | collective-permute-start | bytes 196616 | tf_op jit(solution)/shard_map/ppermute | solution.py:18
  14.0 8.2 %collective-permute-start.9 = (bf16[4,32,256]{2,1,0:T(8,128)(2,1)S(1)}, bf16[4,32,256]{2,1,0:T(8,128)(2,1)S(1)}, u32[]{:S(2)}, u32[]{:S(2)}) collective-permute-start(bf16[4,32,256]{2,1,0:T(8,128)(2,1)S(1)} %get-tuple-element.58.refs_0_), channel_id=1, source_target_pairs={{0,2},{1,3},{2,0},{3,1},{4,6},{5,7},{6,4},{7,5},{8,10},{9,11},{10,... | collective-permute-start | bytes 196616 | tf_op jit(solution)/shard_map/ppermute | solution.py:18
  22.3 5.1 %collective-permute-start.11 = (bf16[4,96,256]{2,1,0:T(8,128)(2,1)S(1)}, bf16[4,96,256]{2,1,0:T(8,128)(2,1)S(1)}, u32[]{:S(2)}, u32[]{:S(2)}) collective-permute-start(bf16[4,96,256]{2,1,0:T(8,128)(2,1)S(1)} %get-tuple-element.50), channel_id=1, source_target_pairs={{4,0},{8,4},{12,8},{16,12},{20,16},{24,20},{28,24},{5,1},{9,5},{13... | collective-permute-start | bytes 589832 | tf_op jit(solution)/shard_map/ppermute | solution.py:24
  24.2 11.9 %collective-permute-start.4 = (bf16[4,96,256]{2,1,0:T(8,128)(2,1)S(1)}, bf16[4,96,256]{2,1,0:T(8,128)(2,1)S(1)}, u32[]{:S(2)}, u32[]{:S(2)}) collective-permute-start(bf16[4,96,256]{2,1,0:T(8,128)(2,1)S(1)} %get-tuple-element.43), channel_id=1, source_target_pairs={{0,4},{4,8},{8,12},{12,16},{16,20},{20,24},{24,28},{1,5},{5,9},{9,... | collective-permute-start | bytes 589832 | tf_op jit(solution)/shard_map/ppermute | solution.py:24
  31.8 14.7 %collective-permute-start.12 = (bf16[4,96,256]{2,1,0:T(8,128)(2,1)S(1)}, bf16[4,96,256]{2,1,0:T(8,128)(2,1)S(1)}, u32[]{:S(2)}, u32[]{:S(2)}) collective-permute-start(bf16[4,96,256]{2,1,0:T(8,128)(2,1)S(1)} %get-tuple-element.52), channel_id=1, source_target_pairs={{0,4},{4,8},{8,12},{12,16},{16,20},{20,24},{24,28},{1,5},{5,9},{9,... | collective-permute-start | bytes 589832 | tf_op jit(solution)/shard_map/ppermute | solution.py:24
  36.2 14.2 %collective-permute-start.5 = (bf16[4,32,256]{2,1,0:T(8,128)(2,1)S(1)}, bf16[4,32,256]{2,1,0:T(8,128)(2,1)S(1)}, u32[]{:S(2)}, u32[]{:S(2)}) collective-permute-start(bf16[4,32,256]{2,1,0:T(8,128)(2,1)S(1)} %get-tuple-element.45), channel_id=1, source_target_pairs={{0,1},{1,2},{2,3},{3,0},{4,5},{5,6},{6,7},{7,4},{8,9},{9,10},{10,1... | collective-permute-start | bytes 196616 | tf_op jit(solution)/shard_map/ppermute | solution.py:18
  36.7 13.7 %collective-permute-start.6 = (bf16[4,32,256]{2,1,0:T(8,128)(2,1)S(1)}, bf16[4,32,256]{2,1,0:T(8,128)(2,1)S(1)}, u32[]{:S(2)}, u32[]{:S(2)}) collective-permute-start(bf16[4,32,256]{2,1,0:T(8,128)(2,1)S(1)} %get-tuple-element.46), channel_id=1, source_target_pairs={{0,2},{1,3},{2,0},{3,1},{4,6},{5,7},{6,4},{7,5},{8,10},{9,11},{10,... | collective-permute-start | bytes 196616 | tf_op jit(solution)/shard_map/ppermute | solution.py:18
  46.4 6.1 %collective-permute-start.7 = (bf16[4,32,256]{2,1,0:T(8,128)(2,1)S(1)}, bf16[4,32,256]{2,1,0:T(8,128)(2,1)S(1)}, u32[]{:S(2)}, u32[]{:S(2)}) collective-permute-start(bf16[4,32,256]{2,1,0:T(8,128)(2,1)S(1)} %get-tuple-element.47), channel_id=1, source_target_pairs={{0,3},{1,0},{2,1},{3,2},{4,7},{5,4},{6,5},{7,6},{8,11},{9,8},{10,9... | collective-permute-start | bytes 196616 | tf_op jit(solution)/shard_map/ppermute | solution.py:18
  46.5 6.0 %collective-permute-start.13 = (bf16[4,32,256]{2,1,0:T(8,128)(2,1)S(1)}, bf16[4,32,256]{2,1,0:T(8,128)(2,1)S(1)}, u32[]{:S(2)}, u32[]{:S(2)}) collective-permute-start(bf16[4,32,256]{2,1,0:T(8,128)(2,1)S(1)} %get-tuple-element.54), channel_id=1, source_target_pairs={{0,1},{1,2},{2,3},{3,0},{4,5},{5,6},{6,7},{7,4},{8,9},{9,10},{10,1... | collective-permute-start | bytes 196616 | tf_op jit(solution)/shard_map/ppermute | solution.py:18
  48.6 7.2 %collective-permute-start.14 = (bf16[4,32,256]{2,1,0:T(8,128)(2,1)S(1)}, bf16[4,32,256]{2,1,0:T(8,128)(2,1)S(1)}, u32[]{:S(2)}, u32[]{:S(2)}) collective-permute-start(bf16[4,32,256]{2,1,0:T(8,128)(2,1)S(1)} %get-tuple-element.55), channel_id=1, source_target_pairs={{0,2},{1,3},{2,0},{3,1},{4,6},{5,7},{6,4},{7,5},{8,10},{9,11},{10,... | collective-permute-start | bytes 196616 | tf_op jit(solution)/shard_map/ppermute | solution.py:18
  50.4 7.5 %collective-permute-start.15 = (bf16[4,32,256]{2,1,0:T(8,128)(2,1)S(1)}, bf16[4,32,256]{2,1,0:T(8,128)(2,1)S(1)}, u32[]{:S(2)}, u32[]{:S(2)}) collective-permute-start(bf16[4,32,256]{2,1,0:T(8,128)(2,1)S(1)} %get-tuple-element.56), channel_id=1, source_target_pairs={{0,3},{1,0},{2,1},{3,2},{4,7},{5,4},{6,5},{7,6},{8,11},{9,8},{10,9... | collective-permute-start | bytes 196616 | tf_op jit(solution)/shard_map/ppermute | solution.py:18

commit v3 on v2

--- a/solution.py
+++ b/solution.py
@@ -7,8 +7,9 @@
 from jax.experimental.pallas import tpu as pltpu
 from jax.sharding import PartitionSpec as P
 
-GROUPS = (8, 4, 2)
+GROUPS = (12, 16, 20)
 ROW_ALIGN = 32
+ORDER_FLOPS = 10**10
 VMEM_LIMIT = 16 * 1024 * 1024
 SMALL_VMEM_LIMIT = 4 * 1024 * 1024
 
@@ -29,11 +30,7 @@
 
 
 def prepare_kernel(
-    tile_rows,
     taps_hbm,
-    sed_hbm,
-    meta_hbm,
-    counts_hbm,
     ry_hbm,
     rx_hbm,
     obs_hbm,
@@ -44,21 +41,17 @@
     ry_ref,
     rx_ref,
     obs_ref,
-    sed_ref,
-    *rest,
+    taps_ref,
+    lines_ref,
+    sems,
 ):
-    plans, (taps_ref, lines_ref, meta_ref, counts_ref, sems) = rest[:-5], rest[-5:]
     bands, terms, axes, tap_count = taps_ref.shape
-    slots = ry_ref.shape[0]
     half = tap_count // 2
     moves = [
         pltpu.make_async_copy(source, target, sems.at[i])
         for i, (source, target) in enumerate(
             (
                 (taps_hbm, taps_ref),
-                (meta_hbm, meta_ref),
-                (counts_hbm, counts_ref),
-                (sed_hbm, sed_ref),
                 (ry_hbm, ry_ref),
                 (rx_hbm, rx_ref),
                 (obs_hbm, obs_ref),
@@ -71,8 +64,7 @@
     lanes = lines_ref.shape[2]
     mirror = lax.broadcasted_iota(jnp.int32, (lanes, lanes), 0) + lax.broadcasted_iota(jnp.int32, (lanes, lanes), 1)
     mirror = (mirror == tap_count - 1).astype(jnp.bfloat16)
-    for move in moves[:3]:
-        move.wait()
+    moves[0].wait()
 
     def one_band(b, carry):
         for t in range(terms):
@@ -97,7 +89,21 @@
         return carry
 
     lax.fori_loop(0, bands, one_band, 0, unroll=True)
-
+    for move in moves[1:]:
+        move.wait()
+
+
+def order_kernel(tile_rows, meta_hbm, counts_hbm, sed_hbm, _, sed_ref, *rest):
+    plans, (meta_ref, counts_ref, sems) = rest[:-3], rest[-3:]
+    slots = (plans[0].shape[0] - 1) // 3
+    moves = [
+        pltpu.make_async_copy(source, target, sems.at[i])
+        for i, (source, target) in enumerate(((meta_hbm, meta_ref), (counts_hbm, counts_ref), (sed_hbm, sed_ref)))
+    ]
+    for move in moves:
+        move.start()
+    for move in moves:
+        move.wait()
     mine = lax.axis_index("shard")
 
     def place(slot, found):
@@ -105,18 +111,15 @@
         col = meta_ref[1, at]
         after = []
         for c, plan_ref in enumerate(plans):
-            hit = col == c
             plan_ref[1 + found[c]] = slot
             plan_ref[1 + slots + found[c]] = meta_ref[0, at] * tile_rows
             plan_ref[1 + 2 * slots + found[c]] = meta_ref[2, at]
-            after.append(found[c] + hit.astype(jnp.int32))
+            after.append(found[c] + (col == c).astype(jnp.int32))
         return tuple(after)
 
     found = lax.fori_loop(0, counts_ref[0, mine], place, (jnp.int32(0),) * len(plans))
     for plan_ref, total in zip(plans, found):
         plan_ref[0] = total
-    for move in moves[3:]:
-        move.wait()
 
 
 def gather_kernel(*refs):
@@ -200,17 +203,16 @@
             place = (band[m], pl.ds(row[m], win_rows), slice(None))
             acc_ref[place] = acc_ref[place] + jnp.where(live[m], window_grad[m], 0.0)
 
-    done = jnp.int32(0)
+    turns = (count + GROUPS[-1] - 1) // GROUPS[-1]
+    fits = [turns * group >= count for group in GROUPS]
     for at, group in enumerate(GROUPS):
-        left = count - done
-        turns = left // group if at < len(GROUPS) - 1 else (left + group - 1) // group
-
-        def turn(i, carry, group=group, done=done):
-            visit(group, done + i * group)
+        taken = jnp.logical_and(fits[at], jnp.logical_not(fits[at - 1])) if at else fits[at]
+
+        def turn(i, carry, group=group):
+            visit(group, i * group)
             return carry
 
-        lax.fori_loop(0, turns, turn, 0)
-        done = done + turns * group
+        lax.fori_loop(0, jnp.where(taken, turns, 0), turn, 0)
 
     for k in range(channels):
         for out_ref, start, rows in ((spill_ref, region_rows, rim_rows), (own_ref, 0, region_rows)):
@@ -267,7 +269,7 @@
         return jax.ShapeDtypeStruct(shape, jnp.bfloat16)
 
     prepared = pl.pallas_call(
-        functools.partial(prepare_kernel, tile_rows),
+        prepare_kernel,
         out_shape=(
             spec(bands, win_rows, terms * win_rows),
             spec(bands, win_rows, terms * win_rows),
@@ -276,35 +278,22 @@
             spec(*resample_rows.shape),
             spec(*resample_cols.shape),
             spec(*observed.shape),
-            jax.ShapeDtypeStruct(sed_weights.shape[::-1], jnp.float32),
-        )
-        + (jax.ShapeDtypeStruct((1 + 3 * slot_count,), jnp.int32),) * col_tiles,
-        in_specs=[anywhere] * 7,
-        out_specs=(vmem,) * 7 + (smem,) * (1 + col_tiles),
+        ),
+        in_specs=[anywhere] * 4,
+        out_specs=(vmem,) * 7,
         scratch_shapes=[
             pltpu.VMEM((bands, terms, 2, tap_count), jnp.float32),
             pltpu.VMEM((bands, 8 * ((2 * terms + 7) // 8), 128), jnp.float32),
-            pltpu.SMEM(exposure_meta.shape, jnp.int32),
-            pltpu.SMEM(slot_counts.shape, jnp.int32),
-            pltpu.SemaphoreType.DMA((7,)),
+            pltpu.SemaphoreType.DMA((4,)),
         ],
         compiler_params=pltpu.CompilerParams(vmem_limit_bytes=VMEM_LIMIT),
-        cost_estimate=pl.CostEstimate(flops=10**8, bytes_accessed=4 * 10**6, transcendentals=0),
+        cost_estimate=pl.CostEstimate(flops=10**8, bytes_accessed=8 * 10**6, transcendentals=0),
     )(
         *(
             pltpu.with_memory_space_constraint(x, pltpu.HBM)
-            for x in (
-                psf_taps.transpose(1, 2, 0, 3),
-                sed_weights.T,
-                exposure_meta,
-                slot_counts,
-                resample_rows,
-                resample_cols,
-                observed,
-            )
+            for x in (psf_taps.transpose(1, 2, 0, 3), resample_rows, resample_cols, observed)
         )
     )
-    plans = prepared[8:]
 
     result = []
     after = prepared[0]
@@ -321,6 +310,28 @@
             cost_estimate=pl.CostEstimate(flops=10**5, bytes_accessed=10**6, transcendentals=0),
         )(*tiles[c], after)
         following = passed_along(rim, "region", -1)
+        if c == 0:
+            sed, *plans = pl.pallas_call(
+                functools.partial(order_kernel, tile_rows),
+                out_shape=(jax.ShapeDtypeStruct(sed_weights.shape[::-1], jnp.float32),)
+                + (jax.ShapeDtypeStruct((1 + 3 * slot_count,), jnp.int32),) * col_tiles,
+                in_specs=[anywhere] * 4,
+                out_specs=(smem,) * (1 + col_tiles),
+                scratch_shapes=[
+                    pltpu.SMEM(exposure_meta.shape, jnp.int32),
+                    pltpu.SMEM(slot_counts.shape, jnp.int32),
+                    pltpu.SemaphoreType.DMA((3,)),
+                ],
+                compiler_params=pltpu.CompilerParams(vmem_limit_bytes=SMALL_VMEM_LIMIT),
+                cost_estimate=pl.CostEstimate(flops=ORDER_FLOPS, bytes_accessed=10**6, transcendentals=0),
+            )(
+                *(
+                    pltpu.with_memory_space_constraint(x, pltpu.HBM)
+                    for x in (exposure_meta, slot_counts, sed_weights.T)
+                ),
+                whole,
+            )
+            after = plans[0]
         own_rows, spill = pl.pallas_call(
             functools.partial(exposures_kernel, terms),
             out_shape=(
@@ -335,8 +346,7 @@
             ],
             compiler_params=pltpu.CompilerParams(vmem_limit_bytes=VMEM_LIMIT),
             cost_estimate=pl.CostEstimate(flops=6 * 10**9, bytes_accessed=6 * 10**6, transcendentals=0),
-        )(plans[c], prepared[7], whole, following, *prepared[:7])
-        after = own_rows
+        )(plans[c], sed, whole, following, *prepared[:7])
         spilled = passed_along(spill, "region", 1)
         total, *given = pl.pallas_call(
             share_kernel,

time: 59.8 us -> 53 us (0.89)
  waiting for transfers between devices: 8.85 us -> 4.64 us
  starting transfers between devices: 35.2 us -> 31.3 us
  Pallas kernels: 12.7 us -> 14.4 us
    ppermute x12, starting transfers between devices: 24.6 us -> 20.6 us  [shifted(): lax.ppermute(block, axis, [(i, (i + distance) % size) for i in range(size)])]
    ppermute x12, waiting for transfers between devices: 8.09 us -> 4.63 us  [shifted(): lax.ppermute(block, axis, [(i, (i + distance) % size) for i in range(size)])]
    pallas_call x2, Pallas kernels: 8.87 us -> 9.83 us  [local(): pl.pallas_call(functools.partial(exposures_kernel, terms), out_shape=(jax...]
    ppermute x4, waiting for transfers between devices: 0.76 us -> 0.01 us  [passed_along(): return lax.ppermute(block, axis, route)]
    pallas_call x1 -> x2, Pallas kernels: 3.63 us -> 4.29 us  [the longest x1 2.71 us: local(): pl.pallas_call(prepare_kernel, out_shape=(spec(bands, win_rows, terms * w...]
  transfers between devices with their start and end apart: 16 -> 16, of which waited for: 5 -> 4; matrix products, arithmetic and copies ran while one was open for 0% -> 0% of each run, Pallas kernels for 22% -> 28%
where the time goes in v3:
time: 53 us; the launch traced here: 52.1 us
  starting transfers between devices  31.3 us (59%)
  Pallas kernels  14.4 us (27%)
  waiting for transfers between devices  4.64 us (9%)
  local copies, waits for them, and re-layouts  0.88 us (2%)
  other arithmetic  0.8 us (2%)
    ppermute x12, starting transfers between devices, shifted(): lax.ppermute(block, axis, [(i, (i + distance) % size) for i in range(size)])  20.6 us
    ppermute x4, starting transfers between devices, passed_along(): return lax.ppermute(block, axis, route)  10.7 us
    pallas_call x2, Pallas kernels, local(): pl.pallas_call(functools.partial(exposures_kernel, terms), out_shape=(jax...  9.83 us
    ppermute x12, waiting for transfers between devices, shifted(): lax.ppermute(block, axis, [(i, (i + distance) % size) for i in range(size)])  4.63 us
    pallas_call x1, Pallas kernels, local(): pl.pallas_call(prepare_kernel, out_shape=(spec(bands, win_rows, terms * w...  2.71 us
    pallas_call x1, Pallas kernels, local(): pl.pallas_call(functools.partial(order_kernel, tile_rows), out_shape=(jax...  1.58 us
  transfers between devices with their start and end apart: 16, of which 4 were waited for; matrix products, arithmetic and copies ran while one was open for 0% of the time, Pallas kernels for 28%

profile of v3, /device:TPU:10, one launch (start us, length us, event | category | flops | bytes accessed | tf_op | source)
XLA Modules:
  0.0 52.1 jit_solution(7368197610608076177)
XLA Ops:
  0.0 0.9 %fusion = (bf16[4,32,256]{2,1,0:T(8,128)(2,1)S(1)}, bf16[4,32,256]{2,1,0:T(8,128)(2,1)S(1)}) fusion(bf16[4,32,512]{2,1,0:T(8,128)(2,1)} %param.8), kind=kLoop, calls=%fused_computation.3 | loop fusion | bytes 262144 | tf_op jit(solution)/shard_map/slice | solution.py:265
  0.9 1.6 %collective-permute-start = (bf16[4,32,256]{2,1,0:T(8,128)(2,1)S(1)}, bf16[4,32,256]{2,1,0:T(8,128)(2,1)S(1)}, u32[]{:S(2)}, u32[]{:S(2)}) collective-permute-start(bf16[4,32,256]{2,1,0:T(8,128)(2,1)S(1)} %get-tuple-element.58.refs_0_), channel_id=1, source_target_pairs={{0,1},{1,2},{2,3},{3,0},{4,5},{5,6},{6,7},{7,4},{8,9},{9,10},{10,1... | collective-permute-start | bytes 196616 | tf_op jit(solution)/shard_map/ppermute | solution.py:19
  2.5 1.2 %collective-permute-start.1 = (bf16[4,32,256]{2,1,0:T(8,128)(2,1)S(1)}, bf16[4,32,256]{2,1,0:T(8,128)(2,1)S(1)}, u32[]{:S(2)}, u32[]{:S(2)}) collective-permute-start(bf16[4,32,256]{2,1,0:T(8,128)(2,1)S(1)} %get-tuple-element.58.refs_0_), channel_id=1, source_target_pairs={{0,2},{1,3},{2,0},{3,1},{4,6},{5,7},{6,4},{7,5},{8,10},{9,11},{10,... | collective-permute-start | bytes 196616 | tf_op jit(solution)/shard_map/ppermute | solution.py:19
  3.7 1.8 %collective-permute-start.2 = (bf16[4,32,256]{2,1,0:T(8,128)(2,1)S(1)}, bf16[4,32,256]{2,1,0:T(8,128)(2,1)S(1)}, u32[]{:S(2)}, u32[]{:S(2)}) collective-permute-start(bf16[4,32,256]{2,1,0:T(8,128)(2,1)S(1)} %get-tuple-element.58.refs_0_), channel_id=1, source_target_pairs={{0,3},{1,0},{2,1},{3,2},{4,7},{5,4},{6,5},{7,6},{8,11},{9,8},{10,9... | collective-permute-start | bytes 196616 | tf_op jit(solution)/shard_map/ppermute | solution.py:19
  5.6 1.3 %collective-permute-start.10 = (bf16[4,32,256]{2,1,0:T(8,128)(2,1)S(1)}, bf16[4,32,256]{2,1,0:T(8,128)(2,1)S(1)}, u32[]{:S(2)}, u32[]{:S(2)}) collective-permute-start(bf16[4,32,256]{2,1,0:T(8,128)(2,1)S(1)} %get-tuple-element.57.refs_0_), channel_id=1, source_target_pairs={{0,3},{1,0},{2,1},{3,2},{4,7},{5,4},{6,5},{7,6},{8,11},{9,8},{10,9... | collective-permute-start | bytes 196616 | tf_op jit(solution)/shard_map/ppermute | solution.py:19
  6.9 0.7 %collective-permute-start.8 = (bf16[4,32,256]{2,1,0:T(8,128)(2,1)S(1)}, bf16[4,32,256]{2,1,0:T(8,128)(2,1)S(1)}, u32[]{:S(2)}, u32[]{:S(2)}) collective-permute-start(bf16[4,32,256]{2,1,0:T(8,128)(2,1)S(1)} %get-tuple-element.57.refs_0_), channel_id=1, source_target_pairs={{0,1},{1,2},{2,3},{3,0},{4,5},{5,6},{6,7},{7,4},{8,9},{9,10},{10,1... | collective-permute-start | bytes 196616 | tf_op jit(solution)/shard_map/ppermute | solution.py:19
  7.6 2.7 %shard_map.82 = (bf16[6,128,384]{2,1,0:T(8,128)(2,1)S(1)}, bf16[6,128,384]{2,1,0:T(8,128)(2,1)S(1)}, bf16[6,256,768]{2,1,0:T(8,128)(2,1)S(1)}, bf16[6,256,768]{2...) custom-call(f32[6,3,2,25]{3,2,1,0:T(2,128)} %bitcast.2, ...), custom_call_target="tpu_custom_call" | custom-call | flops 100000000 | bytes 8000000 | tf_op jit(solution)/shard_map/pallas_call | solution.py:271
  10.3 0.0 collective-permute-done.refs_1_
  10.3 2.2 %collective-permute-start.9 = (bf16[4,32,256]{2,1,0:T(8,128)(2,1)S(1)}, bf16[4,32,256]{2,1,0:T(8,128)(2,1)S(1)}, u32[]{:S(2)}, u32[]{:S(2)}) collective-permute-start(bf16[4,32,256]{2,1,0:T(8,128)(2,1)S(1)} %get-tuple-element.57.refs_0_), channel_id=1, source_target_pairs={{0,2},{1,3},{2,0},{3,1},{4,6},{5,7},{6,4},{7,5},{8,10},{9,11},{10,... | collective-permute-start | bytes 196616 | tf_op jit(solution)/shard_map/ppermute | solution.py:19
  12.5 0.0 collective-permute-done.1.refs_2_
  12.5 0.0 collective-permute-done.2.refs_3_
  12.6 1.9 %collective-permute-start.3 = (bf16[4,96,256]{2,1,0:T(8,128)(2,1)S(1)}, bf16[4,96,256]{2,1,0:T(8,128)(2,1)S(1)}, u32[]{:S(2)}, u32[]{:S(2)}) collective-permute-start(bf16[4,96,256]{2,1,0:T(8,128)(2,1)S(1)} %get-tuple-element.35), channel_id=1, source_target_pairs={{4,0},{8,4},{12,8},{16,12},{20,16},{24,20},{28,24},{5,1},{9,5},{13... | collective-permute-start | bytes 589832 | tf_op jit(solution)/shard_map/ppermute | solution.py:25
  14.5 1.6 %shard_map.84 = (f32[4,6]{1,0:T(4,128)S(1)}, s32[97]{0:T(128)S(1)}, s32[97]{0:T(128)S(1)}) custom-call(s32[3,128]{1,0:T(4,128)} %meta_hbm.1, s32[1,4]{1,0:T(1,128)} %counts_hbm.1, f32[4,6]{1,0:T(4,128)} %bitcast.3, bf16[4,128,256]{2,1,0:T(8,128)(2,1)S(1)} %get-tuple-element.32._.whole_ref), custom_call_target="tpu_custom_call" | custom-call | flops 10000000000 | bytes 1000000 | tf_op jit(solution)/shard_map/pallas_call | solution.py:314
  16.1 0.0 collective-permute-done.10.refs_3_
  16.1 0.0 collective-permute-done.8.refs_1_
  16.1 0.0 collective-permute-done.9.refs_2_
  16.1 0.1 shard_map.87
  16.2 2.8 %collective-permute-start.11 = (bf16[4,96,256]{2,1,0:T(8,128)(2,1)S(1)}, bf16[4,96,256]{2,1,0:T(8,128)(2,1)S(1)}, u32[]{:S(2)}, u32[]{:S(2)}) collective-permute-start(bf16[4,96,256]{2,1,0:T(8,128)(2,1)S(1)} %get-tuple-element.50), channel_id=1, source_target_pairs={{4,0},{8,4},{12,8},{16,12},{20,16},{24,20},{28,24},{5,1},{9,5},{13... | collective-permute-start | bytes 589832 | tf_op jit(solution)/shard_map/ppermute | solution.py:25
  19.0 0.0 collective-permute-done.3.next_ref
  19.0 4.9 %shard_map.85 = (f32[4,128,256]{2,1,0:T(8,128)S(1)}, bf16[4,96,256]{2,1,0:T(8,128)(2,1)S(1)}) custom-call(s32[97]{0:T(128)S(1)} %get-tuple-element.33.plan_ref.refs_4_, f32[4,6]{1,0:T(4,128)S(1)} %get-tuple-element.34.sed_ref, bf16[4,128,256]{2,1,0:T(8,128)(2,1)S(1)} %get-tuple-element.32._.whole_ref, ...), custom_call_target="tpu_custom_call" | custom-call | flops 6000000000 | bytes 6000000 | tf_op jit(solution)/shard_map/pallas_call | solution.py:335
  23.9 2.3 %collective-permute-start.4 = (bf16[4,96,256]{2,1,0:T(8,128)(2,1)S(1)}, bf16[4,96,256]{2,1,0:T(8,128)(2,1)S(1)}, u32[]{:S(2)}, u32[]{:S(2)}) collective-permute-start(bf16[4,96,256]{2,1,0:T(8,128)(2,1)S(1)} %get-tuple-element.43), channel_id=1, source_target_pairs={{0,4},{4,8},{8,12},{12,16},{16,20},{20,24},{24,28},{1,5},{5,9},{9,... | collective-permute-start | bytes 589832 | tf_op jit(solution)/shard_map/ppermute | solution.py:25
  26.2 0.0 collective-permute-done.11.next_ref
  26.2 4.9 %shard_map.88 = (f32[4,128,256]{2,1,0:T(8,128)S(1)}, bf16[4,96,256]{2,1,0:T(8,128)(2,1)S(1)}) custom-call(s32[97]{0:T(128)S(1)} %get-tuple-element.48.plan_ref, f32[4,6]{1,0:T(4,128)S(1)} %get-tuple-element.34.sed_ref, bf16[4,128,256]{2,1,0:T(8,128)(2,1)S(1)} %get-tuple-element.49.whole_ref, bf16[4,96,256]{2,1,0:T(8,128)(2,1)S(1)} %collective-permute-done.11.next_ref, ...), custom_call_target="tpu_custom_call" | custom-call | flops 6000000000 | bytes 6000000 | tf_op jit(solution)/shard_map/pallas_call | solution.py:335
  31.2 3.7 %collective-permute-start.12 = (bf16[4,96,256]{2,1,0:T(8,128)(2,1)S(1)}, bf16[4,96,256]{2,1,0:T(8,128)(2,1)S(1)}, u32[]{:S(2)}, u32[]{:S(2)}) collective-permute-start(bf16[4,96,256]{2,1,0:T(8,128)(2,1)S(1)} %get-tuple-element.52), channel_id=1, source_target_pairs={{0,4},{4,8},{8,12},{12,16},{16,20},{20,24},{24,28},{1,5},{5,9},{9,... | collective-permute-start | bytes 589832 | tf_op jit(solution)/shard_map/ppermute | solution.py:25
  34.9 0.0 collective-permute-done.4.spilled_ref
  34.9 0.1 shard_map.86
  35.0 4.9 %collective-permute-start.5 = (bf16[4,32,256]{2,1,0:T(8,128)(2,1)S(1)}, bf16[4,32,256]{2,1,0:T(8,128)(2,1)S(1)}, u32[]{:S(2)}, u32[]{:S(2)}) collective-permute-start(bf16[4,32,256]{2,1,0:T(8,128)(2,1)S(1)} %get-tuple-element.45), channel_id=1, source_target_pairs={{0,1},{1,2},{2,3},{3,0},{4,5},{5,6},{6,7},{7,4},{8,9},{9,10},{10,1... | collective-permute-start | bytes 196616 | tf_op jit(solution)/shard_map/ppermute | solution.py:19
  39.8 0.0 collective-permute-start.6
  39.8 1.5 %collective-permute-start.7 = (bf16[4,32,256]{2,1,0:T(8,128)(2,1)S(1)}, bf16[4,32,256]{2,1,0:T(8,128)(2,1)S(1)}, u32[]{:S(2)}, u32[]{:S(2)}) collective-permute-start(bf16[4,32,256]{2,1,0:T(8,128)(2,1)S(1)} %get-tuple-element.47), channel_id=1, source_target_pairs={{0,3},{1,0},{2,1},{3,2},{4,7},{5,4},{6,5},{7,6},{8,11},{9,8},{10,9... | collective-permute-start | bytes 196616 | tf_op jit(solution)/shard_map/ppermute | solution.py:19
  41.4 0.0 collective-permute-done.12.spilled_ref
  41.4 0.1 shard_map.89
  41.5 0.5 %collective-permute-start.13 = (bf16[4,32,256]{2,1,0:T(8,128)(2,1)S(1)}, bf16[4,32,256]{2,1,0:T(8,128)(2,1)S(1)}, u32[]{:S(2)}, u32[]{:S(2)}) collective-permute-start(bf16[4,32,256]{2,1,0:T(8,128)(2,1)S(1)} %get-tuple-element.54), channel_id=1, source_target_pairs={{0,1},{1,2},{2,3},{3,0},{4,5},{5,6},{6,7},{7,4},{8,9},{9,10},{10,1... | collective-permute-start | bytes 196616 | tf_op jit(solution)/shard_map/ppermute | solution.py:19
  42.0 4.7 %collective-permute-start.14 = (bf16[4,32,256]{2,1,0:T(8,128)(2,1)S(1)}, bf16[4,32,256]{2,1,0:T(8,128)(2,1)S(1)}, u32[]{:S(2)}, u32[]{:S(2)}) collective-permute-start(bf16[4,32,256]{2,1,0:T(8,128)(2,1)S(1)} %get-tuple-element.55), channel_id=1, source_target_pairs={{0,2},{1,3},{2,0},{3,1},{4,6},{5,7},{6,4},{7,5},{8,10},{9,11},{10,... | collective-permute-start | bytes 196616 | tf_op jit(solution)/shard_map/ppermute | solution.py:19
  46.7 0.0 collective-permute-done.5
  46.7 0.0 collective-permute-start.15
  46.7 0.5 collective-permute-done.6
  47.2 0.0 collective-permute-done.7
  47.2 3.3 %collective-permute-done.13 = bf16[4,32,256]{2,1,0:T(8,128)(2,1)S(1)} collective-permute-done((bf16[4,32,256]{2,1,0:T(8,128)(2,1)S(1)}, bf16[4,32,256]{2,1,0:T(8,128)(2,1)S(1)}, u32[]{:S(2)}, u32[]{:S(2)}) %collective-permute-start.13) | collective-permute-done | bytes 65568 | tf_op jit(solution)/shard_map/ppermute | solution.py:19
  50.5 0.7 %collective-permute-done.14 = bf16[4,32,256]{2,1,0:T(8,128)(2,1)S(1)} collective-permute-done((bf16[4,32,256]{2,1,0:T(8,128)(2,1)S(1)}, bf16[4,32,256]{2,1,0:T(8,128)(2,1)S(1)}, u32[]{:S(2)}, u32[]{:S(2)}) %collective-permute-start.14) | collective-permute-done | bytes 65568 | tf_op jit(solution)/shard_map/ppermute | solution.py:19
  51.2 0.2 collective-permute-done.15
  51.4 0.7 %pad_maximum_fusion = f32[4,32,512]{2,1,0:T(8,128)} fusion(f32[4,32,256]{2,1,0:T(8,128)S(1)} %convert_add_fusion, f32[4,32,256]{2,1,0:T(8,128)S(1)} %convert_add_fusion.1), kind=kLoop, calls=%fused_computation | loop fusion | flops 65536 | bytes 524288 | tf_op jit(solution)/shard_map/concatenate | solution.py:363
  (3 shorter events, 0.1 us)
Async XLA Ops:
  0.9 9.4 %collective-permute-start = (bf16[4,32,256]{2,1,0:T(8,128)(2,1)S(1)}, bf16[4,32,256]{2,1,0:T(8,128)(2,1)S(1)}, u32[]{:S(2)}, u32[]{:S(2)}) collective-permute-start(bf16[4,32,256]{2,1,0:T(8,128)(2,1)S(1)} %get-tuple-element.58.refs_0_), channel_id=1, source_target_pairs={{0,1},{1,2},{2,3},{3,0},{4,5},{5,6},{6,7},{7,4},{8,9},{9,10},{10,1... | collective-permute-start | bytes 196616 | tf_op jit(solution)/shard_map/ppermute | solution.py:19
  2.5 10.0 %collective-permute-start.1 = (bf16[4,32,256]{2,1,0:T(8,128)(2,1)S(1)}, bf16[4,32,256]{2,1,0:T(8,128)(2,1)S(1)}, u32[]{:S(2)}, u32[]{:S(2)}) collective-permute-start(bf16[4,32,256]{2,1,0:T(8,128)(2,1)S(1)} %get-tuple-element.58.refs_0_), channel_id=1, source_target_pairs={{0,2},{1,3},{2,0},{3,1},{4,6},{5,7},{6,4},{7,5},{8,10},{9,11},{10,... | collective-permute-start | bytes 196616 | tf_op jit(solution)/shard_map/ppermute | solution.py:19
  3.7 8.8 %collective-permute-start.2 = (bf16[4,32,256]{2,1,0:T(8,128)(2,1)S(1)}, bf16[4,32,256]{2,1,0:T(8,128)(2,1)S(1)}, u32[]{:S(2)}, u32[]{:S(2)}) collective-permute-start(bf16[4,32,256]{2,1,0:T(8,128)(2,1)S(1)} %get-tuple-element.58.refs_0_), channel_id=1, source_target_pairs={{0,3},{1,0},{2,1},{3,2},{4,7},{5,4},{6,5},{7,6},{8,11},{9,8},{10,9... | collective-permute-start | bytes 196616 | tf_op jit(solution)/shard_map/ppermute | solution.py:19
  5.6 10.5 %collective-permute-start.10 = (bf16[4,32,256]{2,1,0:T(8,128)(2,1)S(1)}, bf16[4,32,256]{2,1,0:T(8,128)(2,1)S(1)}, u32[]{:S(2)}, u32[]{:S(2)}) collective-permute-start(bf16[4,32,256]{2,1,0:T(8,128)(2,1)S(1)} %get-tuple-element.57.refs_0_), channel_id=1, source_target_pairs={{0,3},{1,0},{2,1},{3,2},{4,7},{5,4},{6,5},{7,6},{8,11},{9,8},{10,9... | collective-permute-start | bytes 196616 | tf_op jit(solution)/shard_map/ppermute | solution.py:19
  6.9 9.2 %collective-permute-start.8 = (bf16[4,32,256]{2,1,0:T(8,128)(2,1)S(1)}, bf16[4,32,256]{2,1,0:T(8,128)(2,1)S(1)}, u32[]{:S(2)}, u32[]{:S(2)}) collective-permute-start(bf16[4,32,256]{2,1,0:T(8,128)(2,1)S(1)} %get-tuple-element.57.refs_0_), channel_id=1, source_target_pairs={{0,1},{1,2},{2,3},{3,0},{4,5},{5,6},{6,7},{7,4},{8,9},{9,10},{10,1... | collective-permute-start | bytes 196616 | tf_op jit(solution)/shard_map/ppermute | solution.py:19
  10.3 5.8 %collective-permute-start.9 = (bf16[4,32,256]{2,1,0:T(8,128)(2,1)S(1)}, bf16[4,32,256]{2,1,0:T(8,128)(2,1)S(1)}, u32[]{:S(2)}, u32[]{:S(2)}) collective-permute-start(bf16[4,32,256]{2,1,0:T(8,128)(2,1)S(1)} %get-tuple-element.57.refs_0_), channel_id=1, source_target_pairs={{0,2},{1,3},{2,0},{3,1},{4,6},{5,7},{6,4},{7,5},{8,10},{9,11},{10,... | collective-permute-start | bytes 196616 | tf_op jit(solution)/shard_map/ppermute | solution.py:19
  12.6 6.4 %collective-permute-start.3 = (bf16[4,96,256]{2,1,0:T(8,128)(2,1)S(1)}, bf16[4,96,256]{2,1,0:T(8,128)(2,1)S(1)}, u32[]{:S(2)}, u32[]{:S(2)}) collective-permute-start(bf16[4,96,256]{2,1,0:T(8,128)(2,1)S(1)} %get-tuple-element.35), channel_id=1, source_target_pairs={{4,0},{8,4},{12,8},{16,12},{20,16},{24,20},{28,24},{5,1},{9,5},{13... | collective-permute-start | bytes 589832 | tf_op jit(solution)/shard_map/ppermute | solution.py:25
  16.2 10.1 %collective-permute-start.11 = (bf16[4,96,256]{2,1,0:T(8,128)(2,1)S(1)}, bf16[4,96,256]{2,1,0:T(8,128)(2,1)S(1)}, u32[]{:S(2)}, u32[]{:S(2)}) collective-permute-start(bf16[4,96,256]{2,1,0:T(8,128)(2,1)S(1)} %get-tuple-element.50), channel_id=1, source_target_pairs={{4,0},{8,4},{12,8},{16,12},{20,16},{24,20},{28,24},{5,1},{9,5},{13... | collective-permute-start | bytes 589832 | tf_op jit(solution)/shard_map/ppermute | solution.py:25
  23.9 11.0 %collective-permute-start.4 = (bf16[4,96,256]{2,1,0:T(8,128)(2,1)S(1)}, bf16[4,96,256]{2,1,0:T(8,128)(2,1)S(1)}, u32[]{:S(2)}, u32[]{:S(2)}) collective-permute-start(bf16[4,96,256]{2,1,0:T(8,128)(2,1)S(1)} %get-tuple-element.43), channel_id=1, source_target_pairs={{0,4},{4,8},{8,12},{12,16},{16,20},{20,24},{24,28},{1,5},{5,9},{9,... | collective-permute-start | bytes 589832 | tf_op jit(solution)/shard_map/ppermute | solution.py:25
  31.2 10.2 %collective-permute-start.12 = (bf16[4,96,256]{2,1,0:T(8,128)(2,1)S(1)}, bf16[4,96,256]{2,1,0:T(8,128)(2,1)S(1)}, u32[]{:S(2)}, u32[]{:S(2)}) collective-permute-start(bf16[4,96,256]{2,1,0:T(8,128)(2,1)S(1)} %get-tuple-element.52), channel_id=1, source_target_pairs={{0,4},{4,8},{8,12},{12,16},{16,20},{20,24},{24,28},{1,5},{5,9},{9,... | collective-permute-start | bytes 589832 | tf_op jit(solution)/shard_map/ppermute | solution.py:25
  35.0 11.7 %collective-permute-start.5 = (bf16[4,32,256]{2,1,0:T(8,128)(2,1)S(1)}, bf16[4,32,256]{2,1,0:T(8,128)(2,1)S(1)}, u32[]{:S(2)}, u32[]{:S(2)}) collective-permute-start(bf16[4,32,256]{2,1,0:T(8,128)(2,1)S(1)} %get-tuple-element.45), channel_id=1, source_target_pairs={{0,1},{1,2},{2,3},{3,0},{4,5},{5,6},{6,7},{7,4},{8,9},{9,10},{10,1... | collective-permute-start | bytes 196616 | tf_op jit(solution)/shard_map/ppermute | solution.py:19
  39.8 7.3 %collective-permute-start.6 = (bf16[4,32,256]{2,1,0:T(8,128)(2,1)S(1)}, bf16[4,32,256]{2,1,0:T(8,128)(2,1)S(1)}, u32[]{:S(2)}, u32[]{:S(2)}) collective-permute-start(bf16[4,32,256]{2,1,0:T(8,128)(2,1)S(1)} %get-tuple-element.46), channel_id=1, source_target_pairs={{0,2},{1,3},{2,0},{3,1},{4,6},{5,7},{6,4},{7,5},{8,10},{9,11},{10,... | collective-permute-start | bytes 196616 | tf_op jit(solution)/shard_map/ppermute | solution.py:19
  39.8 7.3 %collective-permute-start.7 = (bf16[4,32,256]{2,1,0:T(8,128)(2,1)S(1)}, bf16[4,32,256]{2,1,0:T(8,128)(2,1)S(1)}, u32[]{:S(2)}, u32[]{:S(2)}) collective-permute-start(bf16[4,32,256]{2,1,0:T(8,128)(2,1)S(1)} %get-tuple-element.47), channel_id=1, source_target_pairs={{0,3},{1,0},{2,1},{3,2},{4,7},{5,4},{6,5},{7,6},{8,11},{9,8},{10,9... | collective-permute-start | bytes 196616 | tf_op jit(solution)/shard_map/ppermute | solution.py:19
  41.5 9.0 %collective-permute-start.13 = (bf16[4,32,256]{2,1,0:T(8,128)(2,1)S(1)}, bf16[4,32,256]{2,1,0:T(8,128)(2,1)S(1)}, u32[]{:S(2)}, u32[]{:S(2)}) collective-permute-start(bf16[4,32,256]{2,1,0:T(8,128)(2,1)S(1)} %get-tuple-element.54), channel_id=1, source_target_pairs={{0,1},{1,2},{2,3},{3,0},{4,5},{5,6},{6,7},{7,4},{8,9},{9,10},{10,1... | collective-permute-start | bytes 196616 | tf_op jit(solution)/shard_map/ppermute | solution.py:19
  42.0 9.2 %collective-permute-start.14 = (bf16[4,32,256]{2,1,0:T(8,128)(2,1)S(1)}, bf16[4,32,256]{2,1,0:T(8,128)(2,1)S(1)}, u32[]{:S(2)}, u32[]{:S(2)}) collective-permute-start(bf16[4,32,256]{2,1,0:T(8,128)(2,1)S(1)} %get-tuple-element.55), channel_id=1, source_target_pairs={{0,2},{1,3},{2,0},{3,1},{4,6},{5,7},{6,4},{7,5},{8,10},{9,11},{10,... | collective-permute-start | bytes 196616 | tf_op jit(solution)/shard_map/ppermute | solution.py:19
  46.7 4.7 %collective-permute-start.15 = (bf16[4,32,256]{2,1,0:T(8,128)(2,1)S(1)}, bf16[4,32,256]{2,1,0:T(8,128)(2,1)S(1)}, u32[]{:S(2)}, u32[]{:S(2)}) collective-permute-start(bf16[4,32,256]{2,1,0:T(8,128)(2,1)S(1)} %get-tuple-element.56), channel_id=1, source_target_pairs={{0,3},{1,0},{2,1},{3,2},{4,7},{5,4},{6,5},{7,6},{8,11},{9,8},{10,9... | collective-permute-start | bytes 196616 | tf_op jit(solution)/shard_map/ppermute | solution.py:19
